TPU v7x, 256 devices: a whole 4x4x8 slice. The times are simulated.
256 devices in a mesh: inner: 8 (over x, y_hi), outer: 32 (over y_lo, z, core).
Axes of the slice: x: 4, y: 4 (y_hi: 2, y_lo: 2; y = y_hi * 2 + y_lo), z: 8, core: 2. Of those that a mesh axis runs over, the one named last changes fastest.
Arguments:
- queries: bfloat16 [32768, 8192], P(('inner', 'outer')), may hold values from -6 to 6
- keys: bfloat16 [32768, 1024], P(('inner', 'outer')), may hold values from -6 to 6
- values: bfloat16 [32768, 1024], P(('inner', 'outer')), may hold values from -6 to 6
- documents: int32 [32768], P(('inner', 'outer')), may hold values from 0 to 127, never falling along the last dimension, each value on 1 to 512 neighbouring positions
Outputs:
- attended: bfloat16 [32768, 8192], P(('inner', 'outer'))
Inputs may be any that keep to these rules, and one draw needn't show every extreme that they name: `documents`: non-decreasing along the sequence; every document spans 1 to 512 tokens, one exactly 512.
All inputs are finite; a program needn't handle non-finite values.
Results may differ from a plain program's by a relative error of at most 0.0045.
Values may be sent and summed in bfloat16 or wider, within the bound.
A program may use at most 64 MiB of HBM per device.

v0:
```python
import jax
import jax.numpy as jnp
from jax import lax
from jax.sharding import PartitionSpec as P

HEAD_SIZE = 128
REACH = 4


def for_sending(array):
    return jax.tree.map(lambda a: a.astype(jnp.bfloat16) if a.dtype == jnp.float32 else a, array)


def from_behind(value, axis, steps):
    count = lax.axis_size(axis)
    pairs = [(source, (source + steps) % count) for source in range(count)]
    return lax.ppermute(value, axis, pairs)


def passed_along(value, axis, steps):
    count = lax.axis_size(axis)
    first, last = (max(0, -steps), min(count, count - steps))
    return lax.ppermute(value, axis, [(source, source + steps) for source in range(first, last)])


def advance(block):
    passed = from_behind((block[0], for_sending(block[1])), "outer", 1)
    carried = passed_along((passed[0], for_sending(passed[1])), "inner", 1)
    first = lax.axis_index("outer") == 0
    return (jnp.where(first, carried[0], passed[0]), jnp.where(first, carried[1], passed[1]))


def local(queries, keys, values, documents):
    tok = queries.shape[0]
    groups = keys.shape[1] // HEAD_SIZE
    group_ratio = queries.shape[1] // (groups * HEAD_SIZE)
    scale = HEAD_SIZE ** (-0.5)
    query_rows = queries.reshape(tok, groups, group_ratio, HEAD_SIZE)
    tags = documents + 1
    positions = jnp.arange(tok, dtype=jnp.int32)
    causal_mask = positions[None, :] <= positions[:, None]

    def attend(state, joined, key_tags, causal):
        summed, top, total = state
        key_part = joined[:, : groups * HEAD_SIZE].reshape(tok, groups, HEAD_SIZE)
        val_part = joined[:, groups * HEAD_SIZE :].reshape(tok, groups, HEAD_SIZE)
        score = (
            jnp.einsum("qgrd,kgd->grqk", query_rows, key_part, preferred_element_type=jnp.float32)
            * scale
        )
        allowed = tags[:, None] == key_tags[None, :]
        if causal:
            allowed = allowed & causal_mask
        score = jnp.where(allowed, score, -1e30)
        new_top = jnp.maximum(top, jnp.max(score, axis=-1))
        weight = jnp.where(allowed, jnp.exp(score - new_top[..., None]), 0.0)
        fade = jnp.exp(top - new_top)
        total = total * fade + jnp.sum(weight, axis=-1)
        product = jnp.einsum(
            "grqk,kgd->qgrd",
            weight.astype(jnp.bfloat16),
            val_part,
            preferred_element_type=jnp.float32,
        )
        summed = summed * jnp.transpose(fade, (2, 0, 1))[..., None] + product
        return (summed, new_top, total)

    joined = jnp.concatenate([keys, values], axis=1)
    state = (
        jnp.zeros((tok, groups, group_ratio, HEAD_SIZE), jnp.float32),
        jnp.full((groups, group_ratio, tok), -1e30, jnp.float32),
        jnp.zeros((groups, group_ratio, tok), jnp.float32),
    )
    state = attend(state, joined, tags, True)
    block = (joined, tags)
    for step in range(REACH):
        block = advance(block)
        kv_now, tags_now = block
        state = attend(state, kv_now, tags_now, False)
    summed, top, total = state
    result = summed / jnp.transpose(total, (2, 0, 1))[..., None]
    return result.reshape(tok, groups * group_ratio * HEAD_SIZE).astype(jnp.bfloat16)


def solution(mesh):
    in_specs = (
        P(("inner", "outer"), None),
        P(("inner", "outer"), None),
        P(("inner", "outer"), None),
        P(("inner", "outer")),
    )
    out_specs = P(("inner", "outer"), None)
    return jax.shard_map(local, mesh=mesh, in_specs=in_specs, out_specs=out_specs, check_vma=False)
```

profile of v0, /device:TPU:6, one launch (start us, length us, event | category | flops | bytes accessed | tf_op | source)
XLA Modules:
  0.0 156.0 jit_solution(3940292220566868623)
XLA Ops:
  2.5 13.2 %collective-permute-done.2 = bf16[128,2048]{0,1:T(8,128)(2,1)S(1)} collective-permute-done((bf16[128,2048]{0,1:T(8,128)(2,1)S(1)}, bf16[128,2048]{0,1:T(8,128)(2,1)S(1)}, u32[]{:S(2)}, u32[]{:S(2)}) %collective-permute-start.2) | collective-permute-done | bytes 524320 | tf_op jit(solution)/shard_map/ppermute | solution.py:17
  15.7 4.8 %collective-permute-start.3 = (bf16[128,2048]{0,1:T(8,128)(2,1)S(1)}, bf16[128,2048]{0,1:T(8,128)(2,1)}, u32[]{:S(2)}, u32[]{:S(2)}) collective-permute-start(bf16[128,2048]{0,1:T(8,128)(2,1)S(1)} %collective-permute-done.2), channel_id=1, source_target_pairs={{0,32},{32,64},{64,96},{96,128},{128,160},{160,192},{192,224},{1,3... | collective-permute-start | bytes 1572872 | tf_op jit(solution)/shard_map/ppermute | solution.py:23
  20.5 8.8 %collective-permute-done.3 = bf16[128,2048]{0,1:T(8,128)(2,1)} collective-permute-done((bf16[128,2048]{0,1:T(8,128)(2,1)S(1)}, bf16[128,2048]{0,1:T(8,128)(2,1)}, u32[]{:S(2)}, u32[]{:S(2)}) %collective-permute-start.3) | collective-permute-done | bytes 524320 | tf_op jit(solution)/shard_map/ppermute | solution.py:23
  31.7 9.5 %collective-permute-done = s32[128]{0:T(128)S(1)} collective-permute-done((s32[128]{0:T(128)S(1)}, s32[128]{0:T(128)S(1)}, u32[]{:S(2)}, u32[]{:S(2)}) %collective-permute-start) | collective-permute-done | bytes 544 | tf_op jit(solution)/shard_map/ppermute | solution.py:17
  41.2 3.9 %collective-permute-start.1 = (s32[128]{0:T(128)S(1)}, s32[128]{0:T(128)S(1)}, u32[]{:S(2)}, u32[]{:S(2)}) collective-permute-start(s32[128]{0:T(128)S(1)} %collective-permute-done), channel_id=1, source_target_pairs={{0,32},{32,64},{64,96},{96,128},{128,160},{160,192},{192,224},{1,3... | collective-permute-start | bytes 1544 | tf_op jit(solution)/shard_map/ppermute | solution.py:23
  45.1 3.9 %collective-permute-done.1 = s32[128]{0:T(128)S(1)} collective-permute-done((s32[128]{0:T(128)S(1)}, s32[128]{0:T(128)S(1)}, u32[]{:S(2)}, u32[]{:S(2)}) %collective-permute-start.1) | collective-permute-done | bytes 544 | tf_op jit(solution)/shard_map/ppermute | solution.py:23
  49.1 5.1 %collective-permute-done.4 = s32[128]{0:T(128)S(1)} collective-permute-done((s32[128]{0:T(128)S(1)}, s32[128]{0:T(128)S(1)}, u32[]{:S(2)}, u32[]{:S(2)}) %collective-permute-start.4) | collective-permute-done | bytes 544 | tf_op jit(solution)/shard_map/ppermute | solution.py:17
  54.1 3.0 %collective-permute-start.5 = (s32[128]{0:T(128)S(1)}, s32[128]{0:T(128)S(1)}, u32[]{:S(2)}, u32[]{:S(2)}) collective-permute-start(s32[128]{0:T(128)S(1)} %collective-permute-done.4), channel_id=1, source_target_pairs={{0,32},{32,64},{64,96},{96,128},{128,160},{160,192},{192,224},{1,3... | collective-permute-start | bytes 1544 | tf_op jit(solution)/shard_map/ppermute | solution.py:23
  57.2 1.9 %collective-permute-start.7 = (bf16[128,2048]{0,1:T(8,128)(2,1)S(1)}, bf16[128,2048]{0,1:T(8,128)(2,1)S(1)}, u32[]{:S(2)}, u32[]{:S(2)}) collective-permute-start(bf16[128,2048]{0,1:T(8,128)(2,1)S(1)} %collective-permute-done.6), channel_id=1, source_target_pairs={{0,32},{32,64},{64,96},{96,128},{128,160},{160,192},{192,224},{1,3... | collective-permute-start | bytes 1572872 | tf_op jit(solution)/shard_map/ppermute | solution.py:23
  59.1 2.9 %collective-permute-done.5 = s32[128]{0:T(128)S(1)} collective-permute-done((s32[128]{0:T(128)S(1)}, s32[128]{0:T(128)S(1)}, u32[]{:S(2)}, u32[]{:S(2)}) %collective-permute-start.5) | collective-permute-done | bytes 544 | tf_op jit(solution)/shard_map/ppermute | solution.py:23
  62.0 5.1 %collective-permute-done.8 = s32[128]{0:T(128)S(1)} collective-permute-done((s32[128]{0:T(128)S(1)}, s32[128]{0:T(128)S(1)}, u32[]{:S(2)}, u32[]{:S(2)}) %collective-permute-start.8) | collective-permute-done | bytes 544 | tf_op jit(solution)/shard_map/ppermute | solution.py:17
  67.1 2.1 %collective-permute-start.9 = (s32[128]{0:T(128)S(1)}, s32[128]{0:T(128)S(1)}, u32[]{:S(2)}, u32[]{:S(2)}) collective-permute-start(s32[128]{0:T(128)S(1)} %collective-permute-done.8), channel_id=1, source_target_pairs={{0,32},{32,64},{64,96},{96,128},{128,160},{160,192},{192,224},{1,3... | collective-permute-start | bytes 1544 | tf_op jit(solution)/shard_map/ppermute | solution.py:23
  69.2 5.7 %collective-permute-done.9 = s32[128]{0:T(128)S(1)} collective-permute-done((s32[128]{0:T(128)S(1)}, s32[128]{0:T(128)S(1)}, u32[]{:S(2)}, u32[]{:S(2)}) %collective-permute-start.9) | collective-permute-done | bytes 544 | tf_op jit(solution)/shard_map/ppermute | solution.py:23
  74.9 5.1 %collective-permute-done.12 = s32[128]{0:T(128)S(1)} collective-permute-done((s32[128]{0:T(128)S(1)}, s32[128]{0:T(128)S(1)}, u32[]{:S(2)}, u32[]{:S(2)}) %collective-permute-start.12) | collective-permute-done | bytes 544 | tf_op jit(solution)/shard_map/ppermute | solution.py:17
  80.0 1.9 %collective-permute-start.13 = (s32[128]{0:T(128)S(1)}, s32[128]{0:T(128)S(1)}, u32[]{:S(2)}, u32[]{:S(2)}) collective-permute-start(s32[128]{0:T(128)S(1)} %collective-permute-done.12), channel_id=1, source_target_pairs={{0,32},{32,64},{64,96},{96,128},{128,160},{160,192},{192,224},{1,3... | collective-permute-start | bytes 1544 | tf_op jit(solution)/shard_map/ppermute | solution.py:23
  82.6 5.2 %collective-permute-done.13 = s32[128]{0:T(128)S(1)} collective-permute-done((s32[128]{0:T(128)S(1)}, s32[128]{0:T(128)S(1)}, u32[]{:S(2)}, u32[]{:S(2)}) %collective-permute-start.13) | collective-permute-done | bytes 544 | tf_op jit(solution)/shard_map/ppermute | solution.py:23
  88.2 2.0 %fusion.6 = (f32[8,8,128]{2,1,0:T(8,128)S(1)}, f32[8,128,128,8]{2,1,3,0:T(8,128)S(1)}) fusion(pred[128,128]{0,1:T(8,128)(4,1)S(1)} %get-tuple-element.24, bf16[128,8,8,128]{3,2,1,0:T(8,128)(2,1)S(1)} %bitcast.243, bf16[128,8,128,1]{2,1,0,3:T(8,128)(2,1)S(1)} %bitcast.251), kind=kOutput, calls=%fused_computation.21 | convolution fusion | flops 271572992 | bytes 6602752 | tf_op jit(solution)/shard_map/qgrd,kgd->grqk/dot_general | solution.py:48
  90.2 8.6 %collective-permute-done.10 = bf16[128,2048]{0,1:T(8,128)(2,1)S(1)} collective-permute-done((bf16[128,2048]{0,1:T(8,128)(2,1)S(1)}, bf16[128,2048]{0,1:T(8,128)(2,1)S(1)}, u32[]{:S(2)}, u32[]{:S(2)}) %collective-permute-start.10) | collective-permute-done | bytes 524320 | tf_op jit(solution)/shard_map/ppermute | solution.py:17
  98.8 1.9 %collective-permute-start.11 = (bf16[128,2048]{0,1:T(8,128)(2,1)S(1)}, bf16[128,2048]{0,1:T(8,128)(2,1)S(1)}, u32[]{:S(2)}, u32[]{:S(2)}) collective-permute-start(bf16[128,2048]{0,1:T(8,128)(2,1)S(1)} %collective-permute-done.10), channel_id=1, source_target_pairs={{0,32},{32,64},{64,96},{96,128},{128,160},{160,192},{192,224},{1,3... | collective-permute-start | bytes 1572872 | tf_op jit(solution)/shard_map/ppermute | solution.py:23
  100.8 2.0 %fusion.7 = (f32[8,8,128]{2,1,0:T(8,128)S(1)}, f32[8,128,128,8]{2,1,3,0:T(8,128)S(1)}) fusion(pred[128,128]{0,1:T(8,128)(4,1)S(1)} %get-tuple-element.28, bf16[128,8,128,1]{0,2,3,1:T(8,128)(2,1)S(1)} %bitcast.257, bf16[128,8,8,128]{3,2,1,0:T(8,128)(2,1)S(1)} %bitcast.244), kind=kOutput, calls=%fused_computation.22 | convolution fusion | flops 271572992 | bytes 6602752 | tf_op jit(solution)/shard_map/qgrd,kgd->grqk/dot_general | solution.py:48
  102.8 9.5 %collective-permute-done.11 = bf16[128,2048]{0,1:T(8,128)(2,1)S(1)} collective-permute-done((bf16[128,2048]{0,1:T(8,128)(2,1)S(1)}, bf16[128,2048]{0,1:T(8,128)(2,1)S(1)}, u32[]{:S(2)}, u32[]{:S(2)}) %collective-permute-start.11) | collective-permute-done | bytes 524320 | tf_op jit(solution)/shard_map/ppermute | solution.py:23
  112.6 2.0 %fusion.8 = (f32[8,8,128]{2,1,0:T(8,128)S(1)}, f32[8,128,128,8]{2,1,3,0:T(8,128)S(1)}) fusion(pred[128,128]{0,1:T(8,128)(4,1)S(1)} %get-tuple-element.25, bf16[128,8,128,1]{0,2,3,1:T(8,128)(2,1)S(1)} %bitcast.258, bf16[128,8,8,128]{3,2,1,0:T(8,128)(2,1)S(1)} %bitcast.245), kind=kOutput, calls=%fused_computation.23 | convolution fusion | flops 271572992 | bytes 6602752 | tf_op jit(solution)/shard_map/qgrd,kgd->grqk/dot_general | solution.py:48
  114.7 8.7 %collective-permute-done.14 = bf16[128,2048]{0,1:T(8,128)(2,1)S(1)} collective-permute-done((bf16[128,2048]{0,1:T(8,128)(2,1)S(1)}, bf16[128,2048]{0,1:T(8,128)(2,1)S(1)}, u32[]{:S(2)}, u32[]{:S(2)}) %collective-permute-start.14) | collective-permute-done | bytes 524320 | tf_op jit(solution)/shard_map/ppermute | solution.py:17
  123.4 1.9 %collective-permute-start.15 = (bf16[128,2048]{0,1:T(8,128)(2,1)S(1)}, bf16[128,2048]{0,1:T(8,128)(2,1)S(1)}, u32[]{:S(2)}, u32[]{:S(2)}) collective-permute-start(bf16[128,2048]{0,1:T(8,128)(2,1)S(1)} %collective-permute-done.14), channel_id=1, source_target_pairs={{0,32},{32,64},{64,96},{96,128},{128,160},{160,192},{192,224},{1,3... | collective-permute-start | bytes 1572872 | tf_op jit(solution)/shard_map/ppermute | solution.py:23
  125.4 2.0 %fusion.9 = (f32[8,8,128]{2,1,0:T(8,128)S(1)}, f32[8,128,128,8]{2,1,3,0:T(8,128)S(1)}) fusion(pred[128,128]{0,1:T(8,128)(4,1)S(1)} %get-tuple-element.26, bf16[128,8,128,1]{0,2,3,1:T(8,128)(2,1)S(1)} %bitcast.259, bf16[128,8,8,128]{3,2,1,0:T(8,128)(2,1)S(1)} %bitcast.246), kind=kOutput, calls=%fused_computation.24 | convolution fusion | flops 271572992 | bytes 6602752 | tf_op jit(solution)/shard_map/qgrd,kgd->grqk/dot_general | solution.py:48
  127.4 9.5 %collective-permute-done.15 = bf16[128,2048]{0,1:T(8,128)(2,1)S(1)} collective-permute-done((bf16[128,2048]{0,1:T(8,128)(2,1)S(1)}, bf16[128,2048]{0,1:T(8,128)(2,1)S(1)}, u32[]{:S(2)}, u32[]{:S(2)}) %collective-permute-start.15) | collective-permute-done | bytes 524320 | tf_op jit(solution)/shard_map/ppermute | solution.py:23
  137.0 2.1 %fusion.10 = (f32[8,8,128]{2,1,0:T(8,128)S(1)}, f32[8,128,128,8]{2,1,3,0:T(8,128)S(1)}) fusion(pred[128,128]{0,1:T(8,128)(4,1)S(1)} %get-tuple-element.27, bf16[128,8,128,1]{0,2,3,1:T(8,128)(2,1)S(1)} %bitcast.256, bf16[128,8,8,128]{3,2,1,0:T(8,128)(2,1)S(1)} %bitcast.247), kind=kOutput, calls=%fused_computation.25 | convolution fusion | flops 271572992 | bytes 6602752 | tf_op jit(solution)/shard_map/qgrd,kgd->grqk/dot_general | solution.py:48
  139.1 1.3 fusion.28
  140.3 2.5 %fusion.11 = (f32[8,8,128]{2,1,0:T(8,128)S(1)}, f32[8,8,128]{2,1,0:T(8,128)S(1)}) fusion(f32[8,128,128,8]{2,1,3,0:T(8,128)S(1)} %get-tuple-element.38, f32[8,8,128]{2,1,0:T(8,128)S(1)} %get-tuple-element.23, pred[128,128]{0,1:T(8,128)(4,1)S(1)} %get-tuple-element.24, f32[8,8,128]{2,1,0:T(8,128)S(1)} %get-tuple-element.12, ...), kind=kLoop, calls=%fused_computation.26 | loop fusion | flops 10469376 | bytes 8552448 | tf_op jit(solution)/shard_map/reduce_sum | solution.py:58
  145.4 2.3 %fusion.15 = (f32[8,8,128]{2,1,0:T(8,128)S(1)}, f32[8,8,128]{2,1,0:T(8,128)S(1)}) fusion(f32[8,128,128,8]{2,1,3,0:T(8,128)S(1)} %get-tuple-element.34, f32[8,8,128]{2,1,0:T(8,128)S(1)} %get-tuple-element.11, pred[128,128]{0,1:T(8,128)(4,1)S(1)} %get-tuple-element.25, f32[8,8,128]{2,1,0:T(8,128)S(1)} %get-tuple-element.10, ...), kind=kLoop, calls=%fused_computation.30 | loop fusion | flops 10469376 | bytes 8552448 | tf_op jit(solution)/shard_map/reduce_sum | solution.py:58
  150.2 2.8 %fusion.1 = bf16[128,8,8,128]{0,3,2,1:T(8,128)(2,1)S(1)} fusion(f32[8,128,8,128]{3,1,2,0:T(8,128)S(1)} %fusion.22, f32[8,128,8,128]{3,1,2,0:T(8,128)S(1)} %fusion.24, f32[8,128,8,128]{3,1,2,0:T(8,128)S(1)} %fusion.26, f32[8,8,128,128]{2,3,1,0:T(8,128)S(1)} %fusion.28, bf16[128,8,128,1]{0,2,3,1:T(8,128)(2,1)S(1)} %bitcast.260, ...), kind=kOutput, calls=%fused_computation.2 | convolution fusion | flops 285212672 | bytes 23576576 | tf_op jit(solution)/shard_map/grqk,kgd->qgrd/dot_general | solution.py:59
  153.1 2.9 %copy.40 = bf16[128,8192]{1,0:T(8,128)(2,1)} copy(bf16[128,8192]{0,1:T(8,128)(2,1)S(1)} %bitcast.250) | data formatting | bytes 4194304 | tf_op jit(solution)/shard_map/convert_element_type | solution.py:82
  (39 shorter events, 11.5 us)
Async XLA Ops:
  0.0 82.6 %copy-start.1 = (bf16[128,1024]{1,0:T(8,128)(2,1)S(1)}, bf16[128,1024]{1,0:T(8,128)(2,1)}, u32[]{:S(2)}) copy-start(bf16[128,1024]{1,0:T(8,128)(2,1)} %param.5) | copy-start | bytes 786436
  0.0 81.9 %copy-start = (bf16[128,8192]{1,0:T(8,128)(2,1)S(1)}, bf16[128,8192]{1,0:T(8,128)(2,1)}, u32[]{:S(2)}) copy-start(bf16[128,8192]{1,0:T(8,128)(2,1)} %param.4) | copy-start | bytes 6291460
  2.5 13.3 %collective-permute-start.2 = (bf16[128,2048]{0,1:T(8,128)(2,1)S(1)}, bf16[128,2048]{0,1:T(8,128)(2,1)S(1)}, u32[]{:S(2)}, u32[]{:S(2)}) collective-permute-start(bf16[128,2048]{0,1:T(8,128)(2,1)S(1)} %pad_maximum_fusion), channel_id=1, source_target_pairs={{0,1},{1,2},{2,3},{3,4},{4,5},{5,6},{6,7},{7,8},{8,9},{9,10},{10,1... | collective-permute-start | bytes 1572872 | tf_op jit(solution)/shard_map/ppermute | solution.py:17
  15.7 13.6 %collective-permute-start.3 = (bf16[128,2048]{0,1:T(8,128)(2,1)S(1)}, bf16[128,2048]{0,1:T(8,128)(2,1)}, u32[]{:S(2)}, u32[]{:S(2)}) collective-permute-start(bf16[128,2048]{0,1:T(8,128)(2,1)S(1)} %collective-permute-done.2), channel_id=1, source_target_pairs={{0,32},{32,64},{64,96},{96,128},{128,160},{160,192},{192,224},{1,3... | collective-permute-start | bytes 1572872 | tf_op jit(solution)/shard_map/ppermute | solution.py:23
  30.4 26.8 %collective-permute-start.6 = (bf16[128,2048]{0,1:T(8,128)(2,1)S(1)}, bf16[128,2048]{0,1:T(8,128)(2,1)S(1)}, u32[]{:S(2)}, u32[]{:S(2)}) collective-permute-start(bf16[128,2048]{0,1:T(8,128)(2,1)S(1)} %broadcast_select_fusion.3), channel_id=1, source_target_pairs={{0,1},{1,2},{2,3},{3,4},{4,5},{5,6},{6,7},{7,8},{8,9},{9,10},{10,1... | collective-permute-start | bytes 1572872 | tf_op jit(solution)/shard_map/ppermute | solution.py:17
  31.1 10.1 %collective-permute-start = (s32[128]{0:T(128)S(1)}, s32[128]{0:T(128)S(1)}, u32[]{:S(2)}, u32[]{:S(2)}) collective-permute-start(s32[128]{0:T(128)S(1)} %broadcast_add_fusion), channel_id=1, source_target_pairs={{0,1},{1,2},{2,3},{3,4},{4,5},{5,6},{6,7},{7,8},{8,9},{9,10},{10,1... | collective-permute-start | bytes 1544 | tf_op jit(solution)/shard_map/ppermute | solution.py:17
  41.2 7.8 %collective-permute-start.1 = (s32[128]{0:T(128)S(1)}, s32[128]{0:T(128)S(1)}, u32[]{:S(2)}, u32[]{:S(2)}) collective-permute-start(s32[128]{0:T(128)S(1)} %collective-permute-done), channel_id=1, source_target_pairs={{0,32},{32,64},{64,96},{96,128},{128,160},{160,192},{192,224},{1,3... | collective-permute-start | bytes 1544 | tf_op jit(solution)/shard_map/ppermute | solution.py:23
  49.1 5.1 %collective-permute-start.4 = (s32[128]{0:T(128)S(1)}, s32[128]{0:T(128)S(1)}, u32[]{:S(2)}, u32[]{:S(2)}) collective-permute-start(s32[128]{0:T(128)S(1)} %broadcast_select_fusion.7), channel_id=1, source_target_pairs={{0,1},{1,2},{2,3},{3,4},{4,5},{5,6},{6,7},{7,8},{8,9},{9,10},{10,1... | collective-permute-start | bytes 1544 | tf_op jit(solution)/shard_map/ppermute | solution.py:17
  54.1 7.9 %collective-permute-start.5 = (s32[128]{0:T(128)S(1)}, s32[128]{0:T(128)S(1)}, u32[]{:S(2)}, u32[]{:S(2)}) collective-permute-start(s32[128]{0:T(128)S(1)} %collective-permute-done.4), channel_id=1, source_target_pairs={{0,32},{32,64},{64,96},{96,128},{128,160},{160,192},{192,224},{1,3... | collective-permute-start | bytes 1544 | tf_op jit(solution)/shard_map/ppermute | solution.py:23
  57.2 30.7 %collective-permute-start.7 = (bf16[128,2048]{0,1:T(8,128)(2,1)S(1)}, bf16[128,2048]{0,1:T(8,128)(2,1)S(1)}, u32[]{:S(2)}, u32[]{:S(2)}) collective-permute-start(bf16[128,2048]{0,1:T(8,128)(2,1)S(1)} %collective-permute-done.6), channel_id=1, source_target_pairs={{0,32},{32,64},{64,96},{96,128},{128,160},{160,192},{192,224},{1,3... | collective-permute-start | bytes 1572872 | tf_op jit(solution)/shard_map/ppermute | solution.py:23
  62.0 5.1 %collective-permute-start.8 = (s32[128]{0:T(128)S(1)}, s32[128]{0:T(128)S(1)}, u32[]{:S(2)}, u32[]{:S(2)}) collective-permute-start(s32[128]{0:T(128)S(1)} %broadcast_select_fusion.6), channel_id=1, source_target_pairs={{0,1},{1,2},{2,3},{3,4},{4,5},{5,6},{6,7},{7,8},{8,9},{9,10},{10,1... | collective-permute-start | bytes 1544 | tf_op jit(solution)/shard_map/ppermute | solution.py:17
  67.1 7.8 %collective-permute-start.9 = (s32[128]{0:T(128)S(1)}, s32[128]{0:T(128)S(1)}, u32[]{:S(2)}, u32[]{:S(2)}) collective-permute-start(s32[128]{0:T(128)S(1)} %collective-permute-done.8), channel_id=1, source_target_pairs={{0,32},{32,64},{64,96},{96,128},{128,160},{160,192},{192,224},{1,3... | collective-permute-start | bytes 1544 | tf_op jit(solution)/shard_map/ppermute | solution.py:23
  74.9 5.1 %collective-permute-start.12 = (s32[128]{0:T(128)S(1)}, s32[128]{0:T(128)S(1)}, u32[]{:S(2)}, u32[]{:S(2)}) collective-permute-start(s32[128]{0:T(128)S(1)} %broadcast_select_fusion.5), channel_id=1, source_target_pairs={{0,1},{1,2},{2,3},{3,4},{4,5},{5,6},{6,7},{7,8},{8,9},{9,10},{10,1... | collective-permute-start | bytes 1544 | tf_op jit(solution)/shard_map/ppermute | solution.py:17
  80.0 7.8 %collective-permute-start.13 = (s32[128]{0:T(128)S(1)}, s32[128]{0:T(128)S(1)}, u32[]{:S(2)}, u32[]{:S(2)}) collective-permute-start(s32[128]{0:T(128)S(1)} %collective-permute-done.12), channel_id=1, source_target_pairs={{0,32},{32,64},{64,96},{96,128},{128,160},{160,192},{192,224},{1,3... | collective-permute-start | bytes 1544 | tf_op jit(solution)/shard_map/ppermute | solution.py:23
  87.9 10.9 %collective-permute-start.10 = (bf16[128,2048]{0,1:T(8,128)(2,1)S(1)}, bf16[128,2048]{0,1:T(8,128)(2,1)S(1)}, u32[]{:S(2)}, u32[]{:S(2)}) collective-permute-start(bf16[128,2048]{0,1:T(8,128)(2,1)S(1)} %broadcast_select_fusion.2), channel_id=1, source_target_pairs={{0,1},{1,2},{2,3},{3,4},{4,5},{5,6},{6,7},{7,8},{8,9},{9,10},{10,1... | collective-permute-start | bytes 1572872 | tf_op jit(solution)/shard_map/ppermute | solution.py:17
  98.8 13.5 %collective-permute-start.11 = (bf16[128,2048]{0,1:T(8,128)(2,1)S(1)}, bf16[128,2048]{0,1:T(8,128)(2,1)S(1)}, u32[]{:S(2)}, u32[]{:S(2)}) collective-permute-start(bf16[128,2048]{0,1:T(8,128)(2,1)S(1)} %collective-permute-done.10), channel_id=1, source_target_pairs={{0,32},{32,64},{64,96},{96,128},{128,160},{160,192},{192,224},{1,3... | collective-permute-start | bytes 1572872 | tf_op jit(solution)/shard_map/ppermute | solution.py:23
  112.3 11.1 %collective-permute-start.14 = (bf16[128,2048]{0,1:T(8,128)(2,1)S(1)}, bf16[128,2048]{0,1:T(8,128)(2,1)S(1)}, u32[]{:S(2)}, u32[]{:S(2)}) collective-permute-start(bf16[128,2048]{0,1:T(8,128)(2,1)S(1)} %broadcast_select_fusion.1), channel_id=1, source_target_pairs={{0,1},{1,2},{2,3},{3,4},{4,5},{5,6},{6,7},{7,8},{8,9},{9,10},{10,1... | collective-permute-start | bytes 1572872 | tf_op jit(solution)/shard_map/ppermute | solution.py:17
  123.4 13.5 %collective-permute-start.15 = (bf16[128,2048]{0,1:T(8,128)(2,1)S(1)}, bf16[128,2048]{0,1:T(8,128)(2,1)S(1)}, u32[]{:S(2)}, u32[]{:S(2)}) collective-permute-start(bf16[128,2048]{0,1:T(8,128)(2,1)S(1)} %collective-permute-done.14), channel_id=1, source_target_pairs={{0,32},{32,64},{64,96},{96,128},{128,160},{160,192},{192,224},{1,3... | collective-permute-start | bytes 1572872 | tf_op jit(solution)/shard_map/ppermute | solution.py:23
where the time goes:
time: 157 us; the launch traced here: 156 us
  waiting for transfers between devices  101 us (64%)
  starting transfers between devices  22.6 us (14%)
  matrix products  17.9 us (11%)
  other arithmetic  8.29 us (5%)
  local copies, waits for them, and re-layouts  6.08 us (4%)
    ppermute x8, waiting for transfers between devices, from_behind(): return lax.ppermute(value, axis, pairs)  55.2 us
    ppermute x8, waiting for transfers between devices, passed_along(): lax.ppermute(value, axis, [(source, source + steps) for source in range(f...  45.6 us
    ppermute x8, starting transfers between devices, passed_along(): lax.ppermute(value, axis, [(source, source + steps) for source in range(f...  21.4 us
    dot_general x5, matrix products, attend(): jnp.einsum('qgrd,kgd->grqk', query_rows, key_part, preferred_element_type...  10.1 us
    dot_general x5, matrix products, attend(): jnp.einsum('grqk,kgd->qgrd', weight.astype(jnp.bfloat16), val_part, prefe...  7.8 us
    reduce_sum x3, other arithmetic, attend(): total = total * fade + jnp.sum(weight, axis=-1)  6.09 us
  transfers between devices with their start and end apart: 16, of which 14 were waited for; matrix products, arithmetic and copies ran while one was open for 6% of the time, Pallas kernels for 0%

commit v1 on v0

v1 whole, which is shorter than its diff:
```python
import functools

import jax
import jax.numpy as jnp
from jax import lax
from jax.experimental import pallas as pl
from jax.experimental.pallas import tpu as pltpu
from jax.sharding import PartitionSpec as P

MESH = pl.DeviceIdType.MESH
HEAD = 128
GROUPS = 8
RATIO = 8
TOK = 128
OWN = 4
AHEAD = 3
MASKED = -1e30
LINK, RELAY, PAIR_NEAR, PAIR_FAR = range(4)
LOG2E = 1.4426950408889634


def kernel(n, outer, q_hbm, k_hbm, v_hbm, doc_ref, o_hbm, kv, tag, qv, ov, bias, in_sem, q_sem, o_sem, send, recv, tsend, trecv):
    b = lax.axis_index("inner") * outer + lax.axis_index("outer")
    core = lax.rem(b, 2)
    sibling = b + 1 - 2 * core
    after = lax.rem(b + 2, n)
    before = lax.rem(b + n - 2, n)

    def at(device):
        return (device // outer, lax.rem(device, outer))

    def load(g):
        cols = pl.ds(pl.multiple_of(g * HEAD, HEAD), HEAD)
        return (
            pltpu.make_async_copy(k_hbm.at[:, cols], kv.at[g, OWN, pl.ds(0, TOK)], in_sem.at[g, 0]),
            pltpu.make_async_copy(v_hbm.at[:, cols], kv.at[g, OWN, pl.ds(TOK, TOK)], in_sem.at[g, 1]),
        )

    def load_q(g):
        cols = pl.ds(pl.multiple_of(g * RATIO * HEAD, HEAD), RATIO * HEAD)
        return pltpu.make_async_copy(q_hbm.at[:, cols], qv.at[g], q_sem.at[g])

    def store(g):
        cols = pl.ds(pl.multiple_of(g * RATIO * HEAD, HEAD), RATIO * HEAD)
        return pltpu.make_async_copy(ov.at[g], o_hbm.at[:, cols], o_sem.at[g])

    near_src = OWN - 2 * core
    far_src = 2 - 2 * core
    routes = {
        LINK: (OWN, 2, after),
        RELAY: (2, 0, after),
        PAIR_NEAR: (near_src, 3, sibling),
        PAIR_FAR: (far_src, 1, sibling),
    }

    def move(kind, g):
        src, dst, device = routes[kind]
        return pltpu.make_async_remote_copy(
            src_ref=kv.at[g, src],
            dst_ref=kv.at[g, dst],
            send_sem=send.at[kind, g],
            recv_sem=recv.at[kind, g],
            device_id=at(device),
            device_id_type=MESH,
        )

    def move_tag(kind):
        src, dst, device = routes[kind]
        return pltpu.make_async_remote_copy(
            src_ref=tag.at[src],
            dst_ref=tag.at[dst],
            send_sem=tsend.at[kind],
            recv_sem=trecv.at[kind],
            device_id=at(device),
            device_id_type=MESH,
        )

    for g in range(GROUPS):
        for c in load(g):
            c.start()
    for g in range(GROUPS):
        load_q(g).start()

    barrier = pltpu.get_barrier_semaphore()
    pl.semaphore_signal(barrier, inc=1, device_id=at(before), device_id_type=MESH)
    pl.semaphore_signal(barrier, inc=1, device_id=at(sibling), device_id_type=MESH)

    docs = jnp.broadcast_to(doc_ref[...].reshape(1, TOK).astype(jnp.float32), (TOK, TOK))
    tag[OWN] = docs[:16].astype(jnp.bfloat16)
    column = docs.T

    pl.semaphore_wait(barrier, 2)
    move_tag(LINK).start()
    for g in range(AHEAD):
        for c in load(g):
            c.wait()
        move(LINK, g).start()
    move_tag(LINK).wait_recv()
    move_tag(RELAY).start()
    move_tag(PAIR_NEAR).start()
    move_tag(RELAY).wait_recv()
    move_tag(PAIR_FAR).start()
    row = lax.broadcasted_iota(jnp.int32, (TOK, TOK), 0)
    col = lax.broadcasted_iota(jnp.int32, (TOK, TOK), 1)
    bias[:, OWN * TOK :] = jnp.where((column == docs) & (col <= row), 0.0, MASKED)
    move_tag(PAIR_NEAR).wait_recv()
    move_tag(PAIR_FAR).wait_recv()
    for s in range(OWN):
        other = jnp.broadcast_to(tag[s][:1].astype(jnp.float32), (TOK, TOK))
        bias[:, s * TOK : (s + 1) * TOK] = jnp.where(column == other, 0.0, MASKED)

    ones = jnp.ones((5 * TOK, HEAD), jnp.bfloat16)

    def compute(g):
        load_q(g).wait()
        k = kv[g, :, :TOK, :].reshape(5 * TOK, HEAD)
        va = jnp.concatenate([kv[g, :, TOK:, :].reshape(5 * TOK, HEAD), ones], axis=1)
        for h in range(RATIO):
            q = qv[g, :, h * HEAD : (h + 1) * HEAD]
            s = lax.dot_general(q, k, (((1,), (1,)), ((), ())), preferred_element_type=jnp.float32)
            t = s * (HEAD**-0.5 * LOG2E) + bias[...]
            p = jnp.exp2(t - jnp.max(t, axis=-1, keepdims=True)).astype(jnp.bfloat16)
            acc = jnp.dot(p, va, preferred_element_type=jnp.float32)
            ov[g, :, h * HEAD : (h + 1) * HEAD] = (acc[:, :HEAD] / acc[:, HEAD:]).astype(jnp.bfloat16)
        store(g).start()

    def step(it, _):
        @pl.when(it < GROUPS)
        def _():
            move(LINK, it).wait_recv()
            move(RELAY, it).start()
            move(PAIR_NEAR, it).start()

        @pl.when(it + AHEAD < GROUPS)
        def _():
            for c in load(it + AHEAD):
                c.wait()
            move(LINK, it + AHEAD).start()

        @pl.when((it >= 1) & (it < GROUPS + 1))
        def _():
            move(RELAY, it - 1).wait_recv()
            move(PAIR_FAR, it - 1).start()

        @pl.when(it >= 2)
        def _():
            move(PAIR_NEAR, it - 2).wait_recv()
            move(PAIR_FAR, it - 2).wait_recv()
            compute(it - 2)

        return 0

    lax.fori_loop(0, GROUPS + 2, step, 0)

    for kind in routes:
        move_tag(kind).wait_send()

    def finish(g, _):
        for kind in routes:
            move(kind, g).wait_send()
        store(g).wait()
        return 0

    lax.fori_loop(0, GROUPS, finish, 0)


def solution(mesh):
    n, outer = mesh.size, mesh.shape["outer"]

    def local(queries, keys, values, documents):
        anywhere = pl.BlockSpec(memory_space=pl.ANY)
        return pl.pallas_call(
            functools.partial(kernel, n, outer),
            out_shape=jax.ShapeDtypeStruct(queries.shape, jnp.bfloat16),
            in_specs=[anywhere, anywhere, anywhere, pl.BlockSpec(memory_space=pltpu.VMEM)],
            out_specs=anywhere,
            scratch_shapes=[
                pltpu.VMEM((GROUPS, 5, 2 * TOK, HEAD), jnp.bfloat16),
                pltpu.VMEM((5, 16, TOK), jnp.bfloat16),
                pltpu.VMEM((GROUPS, TOK, RATIO * HEAD), jnp.bfloat16),
                pltpu.VMEM((GROUPS, TOK, RATIO * HEAD), jnp.bfloat16),
                pltpu.VMEM((TOK, 5 * TOK), jnp.float32),
                pltpu.SemaphoreType.DMA((GROUPS, 2)),
                pltpu.SemaphoreType.DMA((GROUPS,)),
                pltpu.SemaphoreType.DMA((GROUPS,)),
                pltpu.SemaphoreType.DMA((4, GROUPS)),
                pltpu.SemaphoreType.DMA((4, GROUPS)),
                pltpu.SemaphoreType.DMA((4,)),
                pltpu.SemaphoreType.DMA((4,)),
            ],
            name="packed_attention",
            compiler_params=pltpu.CompilerParams(
                collective_id=0, has_side_effects=True, vmem_limit_bytes=60 * 2**20
            ),
            cost_estimate=pl.CostEstimate(flops=2_684_354_560, bytes_accessed=4_718_592, transcendentals=5_242_880),
        )(queries, keys, values, documents)

    row = P(("inner", "outer"), None)
    return jax.shard_map(local, mesh=mesh, in_specs=(row, row, row, P(("inner", "outer"))), out_specs=row, check_vma=False)
```

time: 157 us -> 48.3 us (0.31)
  the two profiles are of different devices: /device:TPU:6 before, /device:TPU:1 now
where the time goes in v1:
time: 48.3 us; the launch traced here: 48.2 us
  Pallas kernels  45.1 us (93%)
  local copies, waits for them, and re-layouts  3.1 us (6%)
    pallas_call x1, Pallas kernels, local(): pl.pallas_call(functools.partial(kernel, n, outer), out_shape=jax.ShapeDt...  45.1 us
    unnamed x1, local copies, waits for them, and re-layouts  3.1 us

profile of v1, /device:TPU:1, one launch (start us, length us, event | category | flops | bytes accessed | tf_op | source)
XLA Modules:
  0.0 48.2 jit_solution(9492783109966609396)
XLA Ops:
  0.0 45.1 %packed_attention.1 = bf16[128,8192]{1,0:T(8,128)(2,1)} custom-call(bf16[128,8192]{1,0:T(8,128)(2,1)} %q_hbm.1, bf16[128,1024]{1,0:T(8,128)(2,1)} %k_hbm.1, bf16[128,1024]{1,0:T(8,128)(2,1)} %v_hbm.1, s32[128]{0:T(128)} %doc_ref.1), custom_call_target="tpu_custom_call" | custom-call | flops 2684354560 | bytes 4718592 | tf_op jit(solution)/shard_map/packed_attention/pallas_call | solution.py:172
  45.1 3.1 %copy.6 = bf16[128,8192]{1,0:T(8,128)(2,1)} copy(bf16[128,8192]{1,0:T(8,128)(2,1)} %packed_attention.1) | data formatting | bytes 4194304

commit v2 on v1

v2 whole, which is shorter than its diff:
```python
import functools

import jax
import jax.numpy as jnp
from jax import lax
from jax.experimental import pallas as pl
from jax.experimental.pallas import tpu as pltpu
from jax.sharding import PartitionSpec as P

MESH = pl.DeviceIdType.MESH
HEAD = 128
GROUPS = 8
RATIO = 8
TOK = 128
OWN = 4
AHEAD = 4
LAG = 3
FIRST = GROUPS - 1
MASKED = -1e30
LINK, RELAY, PAIR_NEAR, PAIR_FAR = range(4)
LOG2E = 1.4426950408889634


def group_columns(g):
    return pl.ds(pl.multiple_of(g * RATIO * HEAD, HEAD), RATIO * HEAD)


def attend(q_at, kv_at, bias, out_at):
    k = kv_at[:, :TOK, :].reshape(5 * TOK, HEAD)
    v = kv_at[:, TOK:, :].reshape(5 * TOK, HEAD)
    v = jnp.concatenate([v, jnp.ones_like(v)], axis=1)
    for h in range(RATIO):
        cols = slice(h * HEAD, (h + 1) * HEAD)
        s = lax.dot_general(q_at[:, cols], k, (((1,), (1,)), ((), ())), preferred_element_type=jnp.float32)
        t = s * (HEAD**-0.5 * LOG2E) + bias[...]
        p = jnp.exp2(t - jnp.max(t, axis=-1, keepdims=True)).astype(jnp.bfloat16)
        acc = jnp.dot(p, v, preferred_element_type=jnp.float32)
        out_at[:, cols] = (acc[:, :HEAD] / acc[:, HEAD:]).astype(jnp.bfloat16)


def first_kernel(n, outer, q_hbm, k_hbm, v_hbm, doc_hbm, part, kv, qv, bias, doc, tag, in_sem, q_sem, d_sem, send, recv, tsend, trecv):
    b = lax.axis_index("inner") * outer + lax.axis_index("outer")
    core = lax.rem(b, 2)
    sibling = b + 1 - 2 * core
    has_next = b < n - 2
    has_prev = b >= 2
    has_two = b >= 4
    after = jnp.minimum(b + 2, n - 2 + core)
    before = jnp.maximum(b - 2, core)

    def at(device):
        return (device // outer, lax.rem(device, outer))

    def load(g):
        cols = pl.ds(pl.multiple_of(g * HEAD, HEAD), HEAD)
        return (
            pltpu.make_async_copy(k_hbm.at[:, cols], kv.at[g, OWN, pl.ds(0, TOK)], in_sem.at[g, 0]),
            pltpu.make_async_copy(v_hbm.at[:, cols], kv.at[g, OWN, pl.ds(TOK, TOK)], in_sem.at[g, 1]),
        )

    def load_q(g):
        return pltpu.make_async_copy(q_hbm.at[:, group_columns(g)], qv.at[g], q_sem.at[g])

    near_src = OWN - 2 * core
    far_src = 2 - 2 * core
    routes = {
        LINK: (OWN, 2, after),
        RELAY: (2, 0, after),
        PAIR_NEAR: (near_src, 3, sibling),
        PAIR_FAR: (far_src, 1, sibling),
    }

    def move(kind, g):
        src, dst, device = routes[kind]
        return pltpu.make_async_remote_copy(
            src_ref=kv.at[g, src],
            dst_ref=kv.at[g, dst],
            send_sem=send.at[kind, g],
            recv_sem=recv.at[kind, g],
            device_id=at(device),
            device_id_type=MESH,
        )

    def move_tag(kind):
        src, dst, device = routes[kind]
        return pltpu.make_async_remote_copy(
            src_ref=tag.at[src],
            dst_ref=tag.at[dst],
            send_sem=tsend.at[kind],
            recv_sem=trecv.at[kind],
            device_id=at(device),
            device_id_type=MESH,
        )

    doc_copy = pltpu.make_async_copy(doc_hbm, doc, d_sem)
    doc_copy.start()
    for g in range(GROUPS):
        for c in load(g):
            c.start()
    for g in range(GROUPS):
        load_q(g).start()

    barrier = pltpu.get_barrier_semaphore()

    @pl.when(has_prev)
    def _():
        pl.semaphore_signal(barrier, inc=1, device_id=at(before), device_id_type=MESH)

    pl.semaphore_signal(barrier, inc=1, device_id=at(sibling), device_id_type=MESH)

    @pl.when(jnp.logical_not(has_two))
    def _():
        kv[:, 0] = jnp.zeros((GROUPS, 2 * TOK, HEAD), jnp.bfloat16)
        tag[0] = jnp.full((16, TOK), -1, jnp.bfloat16)

    @pl.when(jnp.logical_not(has_prev))
    def _():
        kv[:, 2] = jnp.zeros((GROUPS, 2 * TOK, HEAD), jnp.bfloat16)
        tag[2] = jnp.full((16, TOK), -1, jnp.bfloat16)

    doc_copy.wait()
    docs = jnp.broadcast_to(doc[...].reshape(1, TOK).astype(jnp.float32), (TOK, TOK))
    tag[OWN] = docs[:16].astype(jnp.bfloat16)
    column = docs.T

    def when(condition, action):
        pl.when(condition)(action)

    pl.semaphore_wait(barrier, 1 + has_next.astype(jnp.int32))
    when(has_next, lambda: move_tag(LINK).start())
    for g in range(AHEAD):
        for c in load(g):
            c.wait()
        when(has_next, lambda: move(LINK, g).start())
    when(has_prev, lambda: move_tag(LINK).wait_recv())
    when(has_prev & has_next, lambda: move_tag(RELAY).start())
    move_tag(PAIR_NEAR).start()
    row = lax.broadcasted_iota(jnp.int32, (TOK, TOK), 0)
    col = lax.broadcasted_iota(jnp.int32, (TOK, TOK), 1)
    bias[:, OWN * TOK :] = jnp.where((column == docs) & (col <= row), 0.0, MASKED)
    when(has_two, lambda: move_tag(RELAY).wait_recv())
    move_tag(PAIR_FAR).start()
    move_tag(PAIR_NEAR).wait_recv()
    move_tag(PAIR_FAR).wait_recv()
    for s in range(OWN):
        other = jnp.broadcast_to(tag[s][:1].astype(jnp.float32), (TOK, TOK))
        bias[:, s * TOK : (s + 1) * TOK] = jnp.where(column == other, 0.0, MASKED)

    def step(it, _):
        @pl.when(it < GROUPS)
        def _():
            when(has_prev, lambda: move(LINK, it).wait_recv())
            when(has_prev & has_next, lambda: move(RELAY, it).start())
            move(PAIR_NEAR, it).start()

        @pl.when(it + AHEAD < GROUPS)
        def _():
            for c in load(it + AHEAD):
                c.wait()
            when(has_next, lambda: move(LINK, it + AHEAD).start())

        @pl.when((it >= LAG) & (it < GROUPS + LAG))
        def _():
            when(has_two, lambda: move(RELAY, it - LAG).wait_recv())
            move(PAIR_FAR, it - LAG).start()

        @pl.when(it > LAG)
        def _():
            g = it - LAG - 1
            move(PAIR_NEAR, g).wait_recv()
            move(PAIR_FAR, g).wait_recv()
            load_q(g).wait()
            attend(qv.at[g], kv.at[g], bias, part.at[g])

        return 0

    lax.fori_loop(0, FIRST + LAG + 1, step, 0)

    for kind in routes:
        if kind == LINK:
            when(has_next, lambda: move_tag(LINK).wait_send())
        elif kind == RELAY:
            when(has_prev & has_next, lambda: move_tag(RELAY).wait_send())
        else:
            move_tag(kind).wait_send()

    def finish(g, _):
        when(has_next, lambda: move(LINK, g).wait_send())
        when(has_prev & has_next, lambda: move(RELAY, g).wait_send())
        move(PAIR_NEAR, g).wait_send()
        move(PAIR_FAR, g).wait_send()
        return 0

    lax.fori_loop(0, GROUPS, finish, 0)
    for g in range(FIRST, GROUPS):
        load_q(g).wait()
        move(PAIR_NEAR, g).wait_recv()
        move(PAIR_FAR, g).wait_recv()


def last_kernel(part, kv, qv, bias, o_hbm, out, sem):
    def store(g):
        source = part.at[g] if g < FIRST else out.at[g - FIRST]
        return pltpu.make_async_copy(source, o_hbm.at[:, group_columns(g)], sem.at[g])

    for g in range(FIRST):
        store(g).start()
    for g in range(FIRST, GROUPS):
        attend(qv.at[g], kv.at[g], bias, out.at[g - FIRST])
        store(g).start()
    for g in range(GROUPS):
        store(g).wait()


def solution(mesh):
    n, outer = mesh.size, mesh.shape["outer"]

    def local(queries, keys, values, documents):
        anywhere = pl.BlockSpec(memory_space=pl.ANY)
        vmem = pl.BlockSpec(memory_space=pltpu.VMEM)
        arguments = [pltpu.with_memory_space_constraint(x, pltpu.HBM) for x in (queries, keys, values, documents)]
        part, kv, qv, bias = pl.pallas_call(
            functools.partial(first_kernel, n, outer),
            out_shape=(
                pltpu.VMEM((FIRST, TOK, RATIO * HEAD), jnp.bfloat16),
                pltpu.VMEM((GROUPS, 5, 2 * TOK, HEAD), jnp.bfloat16),
                pltpu.VMEM((GROUPS, TOK, RATIO * HEAD), jnp.bfloat16),
                pltpu.VMEM((TOK, 5 * TOK), jnp.float32),
            ),
            in_specs=[anywhere] * 4,
            out_specs=(vmem,) * 4,
            scratch_shapes=[
                pltpu.VMEM((TOK,), jnp.int32),
                pltpu.VMEM((5, 16, TOK), jnp.bfloat16),
                pltpu.SemaphoreType.DMA((GROUPS, 2)),
                pltpu.SemaphoreType.DMA((GROUPS,)),
                pltpu.SemaphoreType.DMA,
                pltpu.SemaphoreType.DMA((4, GROUPS)),
                pltpu.SemaphoreType.DMA((4, GROUPS)),
                pltpu.SemaphoreType.DMA((4,)),
                pltpu.SemaphoreType.DMA((4,)),
            ],
            name="relay_and_attend",
            compiler_params=pltpu.CompilerParams(
                collective_id=0, has_side_effects=True, vmem_limit_bytes=24 * 2**20
            ),
        )(*arguments)
        return pl.pallas_call(
            last_kernel,
            out_shape=jax.ShapeDtypeStruct(queries.shape, jnp.bfloat16),
            in_specs=[vmem] * 4,
            out_specs=anywhere,
            scratch_shapes=[
                pltpu.VMEM((GROUPS - FIRST, TOK, RATIO * HEAD), jnp.bfloat16),
                pltpu.SemaphoreType.DMA((GROUPS,)),
            ],
            name="attend_and_write",
            compiler_params=pltpu.CompilerParams(vmem_limit_bytes=24 * 2**20),
        )(part, kv, qv, bias)

    row = P(("inner", "outer"), None)
    return jax.shard_map(local, mesh=mesh, in_specs=(row, row, row, P(("inner", "outer"))), out_specs=row, check_vma=False)
```

time: 48.3 us -> 41.7 us (0.86)
  the two profiles are of different devices: /device:TPU:1 before, /device:TPU:7 now
where the time goes in v2:
time: 41.7 us; the launch traced here: 41.6 us
  Pallas kernels  41.6 us (100%)
    pallas_call x1, Pallas kernels, local(): pl.pallas_call(functools.partial(first_kernel, n, outer), out_shape=(pltp...  39.2 us
    pallas_call x1, Pallas kernels, local(): pl.pallas_call(last_kernel, out_shape=jax.ShapeDtypeStruct(queries.shape,...  2.33 us

profile of v2, /device:TPU:7, one launch (start us, length us, event | category | flops | bytes accessed | tf_op | source)
XLA Modules:
  0.0 41.6 jit_solution(13858304722659212289)
XLA Ops:
  0.0 39.2 %relay_and_attend.1 = (bf16[7,128,1024]{2,1,0:T(8,128)(2,1)S(1)}, bf16[8,5,256,128]{3,2,1,0:T(8,128)(2,1)S(1)}, bf16[8,128,1024]{2,1,0:T(8,128)(2,1)S(1)}, f32[128,640]{1,0:T(8,128)S(1)}) custom-call(bf16[128,8192]{1,0:T(8,128)(2,1)} %q_hbm.1, bf16[128,1024]{1,0:T(8,128)(2,1)} %k_hbm.1, bf16[128,1024]{1,0:T(8,128)(2,1)} %v_hbm.1, s32[128]{0:T(128)} %doc_hbm.1), custom_call_target="tpu_custom_call" | custom-call | tf_op jit(solution)/shard_map/relay_and_attend/pallas_call | solution.py:222
  39.3 2.3 %attend_and_write.1 = bf16[128,8192]{1,0:T(8,128)(2,1)} custom-call(bf16[7,128,1024]{2,1,0:T(8,128)(2,1)S(1)} %get-tuple-element.9.part, bf16[8,5,256,128]{3,2,1,0:T(8,128)(2,1)S(1)} %get-tuple-element.10.kv, bf16[8,128,1024]{2,1,0:T(8,128)(2,1)S(1)} %get-tuple-element.11.qv, f32[128,640]{1,0:T(8,128)S(1)} %get-tuple-element.12.bias), custom_call_target="tpu_custom_call" | custom-call | tf_op jit(solution)/shard_map/attend_and_write/pallas_call | solution.py:248

commit v3 on v2

--- a/solution.py
+++ b/solution.py
@@ -15,6 +15,8 @@
 OWN = 4
 AHEAD = 4
 LAG = 3
+DIVERT = 6
+KEPT = GROUPS - DIVERT
 FIRST = GROUPS - 1
 MASKED = -1e30
 LINK, RELAY, PAIR_NEAR, PAIR_FAR = range(4)
@@ -38,13 +40,18 @@
         out_at[:, cols] = (acc[:, :HEAD] / acc[:, HEAD:]).astype(jnp.bfloat16)
 
 
-def first_kernel(n, outer, q_hbm, k_hbm, v_hbm, doc_hbm, part, kv, qv, bias, doc, tag, in_sem, q_sem, d_sem, send, recv, tsend, trecv):
+def first_kernel(n, outer, q_hbm, k_hbm, v_hbm, doc_hbm, part, kv, qv, bias, doc, column, tag, mid, in_sem, q_sem, d_sem, send, recv, tsend, trecv, dsend, drecv):
     b = lax.axis_index("inner") * outer + lax.axis_index("outer")
     core = lax.rem(b, 2)
     sibling = b + 1 - 2 * core
     has_next = b < n - 2
     has_prev = b >= 2
     has_two = b >= 4
+    z = lax.rem(b // 2, 8)
+    more_rows = b < n - 16
+    is_source = (z == 6) & more_rows
+    is_middle = (z == 3) & (b >= 16)
+    is_target = (z == 0) & (b >= 16)
     after = jnp.minimum(b + 2, n - 2 + core)
     before = jnp.maximum(b - 2, core)
 
@@ -92,6 +99,29 @@
             device_id_type=MESH,
         )
 
+    def to_middle(m):
+        return pltpu.make_async_remote_copy(
+            src_ref=kv.at[KEPT + m, OWN],
+            dst_ref=mid.at[m],
+            send_sem=dsend.at[0, m],
+            recv_sem=drecv.at[m],
+            device_id=at(jnp.minimum(b + 10, n - 1)),
+            device_id_type=MESH,
+        )
+
+    def from_middle(m):
+        return pltpu.make_async_remote_copy(
+            src_ref=mid.at[m],
+            dst_ref=kv.at[KEPT + m, 0],
+            send_sem=dsend.at[1, m],
+            recv_sem=recv.at[RELAY, KEPT + m],
+            device_id=at(jnp.maximum(b - 6, 0)),
+            device_id_type=MESH,
+        )
+
+    def relays(g):
+        return has_prev & has_next & jnp.logical_not((z == 7) & (g >= KEPT))
+
     doc_copy = pltpu.make_async_copy(doc_hbm, doc, d_sem)
     doc_copy.start()
     for g in range(GROUPS):
@@ -106,6 +136,14 @@
     def _():
         pl.semaphore_signal(barrier, inc=1, device_id=at(before), device_id_type=MESH)
 
+    @pl.when(is_middle)
+    def _():
+        pl.semaphore_signal(barrier, inc=1, device_id=at(jnp.maximum(b - 10, 0)), device_id_type=MESH)
+
+    @pl.when(is_target)
+    def _():
+        pl.semaphore_signal(barrier, inc=1, device_id=at(jnp.minimum(b + 6, n - 1)), device_id_type=MESH)
+
     pl.semaphore_signal(barrier, inc=1, device_id=at(sibling), device_id_type=MESH)
 
     @pl.when(jnp.logical_not(has_two))
@@ -121,48 +159,62 @@
     doc_copy.wait()
     docs = jnp.broadcast_to(doc[...].reshape(1, TOK).astype(jnp.float32), (TOK, TOK))
     tag[OWN] = docs[:16].astype(jnp.bfloat16)
-    column = docs.T
+    column[...] = docs.T
 
     def when(condition, action):
         pl.when(condition)(action)
 
-    pl.semaphore_wait(barrier, 1 + has_next.astype(jnp.int32))
+    pl.semaphore_wait(barrier, 1 + has_next.astype(jnp.int32) + (is_source | is_middle).astype(jnp.int32))
     when(has_next, lambda: move_tag(LINK).start())
-    for g in range(AHEAD):
+    for g in range(GROUPS):
         for c in load(g):
             c.wait()
-        when(has_next, lambda: move(LINK, g).start())
-    when(has_prev, lambda: move_tag(LINK).wait_recv())
-    when(has_prev & has_next, lambda: move_tag(RELAY).start())
-    move_tag(PAIR_NEAR).start()
+        if g < AHEAD:
+            when(has_next, lambda: move(LINK, g).start())
+    for m in range(DIVERT):
+        when(is_source, lambda: to_middle(m).start())
     row = lax.broadcasted_iota(jnp.int32, (TOK, TOK), 0)
     col = lax.broadcasted_iota(jnp.int32, (TOK, TOK), 1)
-    bias[:, OWN * TOK :] = jnp.where((column == docs) & (col <= row), 0.0, MASKED)
-    when(has_two, lambda: move_tag(RELAY).wait_recv())
-    move_tag(PAIR_FAR).start()
-    move_tag(PAIR_NEAR).wait_recv()
-    move_tag(PAIR_FAR).wait_recv()
-    for s in range(OWN):
-        other = jnp.broadcast_to(tag[s][:1].astype(jnp.float32), (TOK, TOK))
-        bias[:, s * TOK : (s + 1) * TOK] = jnp.where(column == other, 0.0, MASKED)
-
+    bias[:, OWN * TOK :] = jnp.where((column[...] == docs) & (col <= row), 0.0, MASKED)
     def step(it, _):
+        @pl.when(it == 0)
+        def _():
+            when(has_prev, lambda: move_tag(LINK).wait_recv())
+            when(has_prev & has_next, lambda: move_tag(RELAY).start())
+            move_tag(PAIR_NEAR).start()
+            when(core == 0, lambda: move_tag(PAIR_FAR).start())
+
         @pl.when(it < GROUPS)
         def _():
             when(has_prev, lambda: move(LINK, it).wait_recv())
-            when(has_prev & has_next, lambda: move(RELAY, it).start())
+            when(relays(it), lambda: move(RELAY, it).start())
             move(PAIR_NEAR, it).start()
-
-        @pl.when(it + AHEAD < GROUPS)
-        def _():
-            for c in load(it + AHEAD):
-                c.wait()
-            when(has_next, lambda: move(LINK, it + AHEAD).start())
+            when(core == 0, lambda: move(PAIR_FAR, it).start())
+
+        when(has_next & (it + AHEAD < GROUPS), lambda: move(LINK, it + AHEAD).start())
+
+        @pl.when(is_middle & (it >= KEPT - 1) & (it < GROUPS - 1))
+        def _():
+            to_middle(it - KEPT + 1).wait_recv()
+            from_middle(it - KEPT + 1).start()
+
+        @pl.when(it == LAG)
+        def _():
+            when(has_two, lambda: move_tag(RELAY).wait_recv())
+            when(core == 1, lambda: move_tag(PAIR_FAR).start())
 
         @pl.when((it >= LAG) & (it < GROUPS + LAG))
         def _():
             when(has_two, lambda: move(RELAY, it - LAG).wait_recv())
-            move(PAIR_FAR, it - LAG).start()
+            when(core == 1, lambda: move(PAIR_FAR, it - LAG).start())
+
+        @pl.when(it == LAG + 1)
+        def _():
+            move_tag(PAIR_NEAR).wait_recv()
+            move_tag(PAIR_FAR).wait_recv()
+            for s in range(OWN):
+                other = jnp.broadcast_to(tag[s][:1].astype(jnp.float32), (TOK, TOK))
+                bias[:, s * TOK : (s + 1) * TOK] = jnp.where(column[...] == other, 0.0, MASKED)
 
         @pl.when(it > LAG)
         def _():
@@ -186,12 +238,15 @@
 
     def finish(g, _):
         when(has_next, lambda: move(LINK, g).wait_send())
-        when(has_prev & has_next, lambda: move(RELAY, g).wait_send())
+        when(relays(g), lambda: move(RELAY, g).wait_send())
         move(PAIR_NEAR, g).wait_send()
         move(PAIR_FAR, g).wait_send()
         return 0
 
     lax.fori_loop(0, GROUPS, finish, 0)
+    for m in range(DIVERT):
+        when(is_source, lambda: to_middle(m).wait_send())
+        when(is_middle, lambda: from_middle(m).wait_send())
     for g in range(FIRST, GROUPS):
         load_q(g).wait()
         move(PAIR_NEAR, g).wait_recv()
@@ -231,7 +286,9 @@
             out_specs=(vmem,) * 4,
             scratch_shapes=[
                 pltpu.VMEM((TOK,), jnp.int32),
+                pltpu.VMEM((TOK, TOK), jnp.float32),
                 pltpu.VMEM((5, 16, TOK), jnp.bfloat16),
+                pltpu.VMEM((DIVERT, 2 * TOK, HEAD), jnp.bfloat16),
                 pltpu.SemaphoreType.DMA((GROUPS, 2)),
                 pltpu.SemaphoreType.DMA((GROUPS,)),
                 pltpu.SemaphoreType.DMA,
@@ -239,6 +296,8 @@
                 pltpu.SemaphoreType.DMA((4, GROUPS)),
                 pltpu.SemaphoreType.DMA((4,)),
                 pltpu.SemaphoreType.DMA((4,)),
+                pltpu.SemaphoreType.DMA((2, DIVERT)),
+                pltpu.SemaphoreType.DMA((DIVERT,)),
             ],
             name="relay_and_attend",
             compiler_params=pltpu.CompilerParams(

time: 41.7 us -> 36.9 us (0.88)
  the two profiles are of different devices: /device:TPU:7 before, /device:TPU:38 now
where the time goes in v3:
time: 36.9 us; the launch traced here: 36.8 us
  Pallas kernels  36.7 us (99%)
    pallas_call x1, Pallas kernels, local(): pl.pallas_call(functools.partial(first_kernel, n, outer), out_shape=(pltp...  34.4 us
    pallas_call x1, Pallas kernels, local(): pl.pallas_call(last_kernel, out_shape=jax.ShapeDtypeStruct(queries.shape,...  2.32 us

profile of v3, /device:TPU:38, one launch (start us, length us, event | category | flops | bytes accessed | tf_op | source)
XLA Modules:
  0.0 36.8 jit_solution(7957217532529986308)
XLA Ops:
  0.0 34.4 %relay_and_attend.1 = (bf16[7,128,1024]{2,1,0:T(8,128)(2,1)S(1)}, bf16[8,5,256,128]{3,2,1,0:T(8,128)(2,1)S(1)}, bf16[8,128,1024]{2,1,0:T(8,128)(2,1)S(1)}, f32[128,640]{1,0:T(8,128)S(1)}) custom-call(bf16[128,8192]{1,0:T(8,128)(2,1)} %q_hbm.1, bf16[128,1024]{1,0:T(8,128)(2,1)} %k_hbm.1, bf16[128,1024]{1,0:T(8,128)(2,1)} %v_hbm.1, s32[128]{0:T(128)} %doc_hbm.1), custom_call_target="tpu_custom_call" | custom-call | tf_op jit(solution)/shard_map/relay_and_attend/pallas_call | solution.py:277
  34.4 2.3 %attend_and_write.1 = bf16[128,8192]{1,0:T(8,128)(2,1)} custom-call(bf16[7,128,1024]{2,1,0:T(8,128)(2,1)S(1)} %get-tuple-element.9.part, bf16[8,5,256,128]{3,2,1,0:T(8,128)(2,1)S(1)} %get-tuple-element.10.kv, bf16[8,128,1024]{2,1,0:T(8,128)(2,1)S(1)} %get-tuple-element.11.qv, f32[128,640]{1,0:T(8,128)S(1)} %get-tuple-element.12.bias), custom_call_target="tpu_custom_call" | custom-call | tf_op jit(solution)/shard_map/attend_and_write/pallas_call | solution.py:307

commit v4 on v3

--- a/solution.py
+++ b/solution.py
@@ -12,10 +12,11 @@
 GROUPS = 8
 RATIO = 8
 TOK = 128
+NEAR = 2
 OWN = 4
 AHEAD = 4
 LAG = 3
-DIVERT = 6
+DIVERT = 8
 KEPT = GROUPS - DIVERT
 FIRST = GROUPS - 1
 MASKED = -1e30
@@ -27,20 +28,41 @@
     return pl.ds(pl.multiple_of(g * RATIO * HEAD, HEAD), RATIO * HEAD)
 
 
-def attend(q_at, kv_at, bias, out_at):
-    k = kv_at[:, :TOK, :].reshape(5 * TOK, HEAD)
-    v = kv_at[:, TOK:, :].reshape(5 * TOK, HEAD)
-    v = jnp.concatenate([v, jnp.ones_like(v)], axis=1)
+def scores(q_at, k, bias, h):
+    q = q_at[:, h * HEAD : (h + 1) * HEAD]
+    s = lax.dot_general(q, k, (((1,), (1,)), ((), ())), preferred_element_type=jnp.float32)
+    return s * (HEAD**-0.5 * LOG2E) + bias
+
+
+def keys_values(kv_at, first, last):
+    k = kv_at[first:last, :TOK, :].reshape((last - first) * TOK, HEAD)
+    v = kv_at[first:last, TOK:, :].reshape((last - first) * TOK, HEAD)
+    return k, jnp.concatenate([v, jnp.ones_like(v)], axis=1)
+
+
+def attend_near(q_at, kv_at, bias, acc_at, top_at):
+    k, v = keys_values(kv_at, NEAR, OWN + 1)
     for h in range(RATIO):
-        cols = slice(h * HEAD, (h + 1) * HEAD)
-        s = lax.dot_general(q_at[:, cols], k, (((1,), (1,)), ((), ())), preferred_element_type=jnp.float32)
-        t = s * (HEAD**-0.5 * LOG2E) + bias[...]
-        p = jnp.exp2(t - jnp.max(t, axis=-1, keepdims=True)).astype(jnp.bfloat16)
-        acc = jnp.dot(p, v, preferred_element_type=jnp.float32)
-        out_at[:, cols] = (acc[:, :HEAD] / acc[:, HEAD:]).astype(jnp.bfloat16)
-
-
-def first_kernel(n, outer, q_hbm, k_hbm, v_hbm, doc_hbm, part, kv, qv, bias, doc, column, tag, mid, in_sem, q_sem, d_sem, send, recv, tsend, trecv, dsend, drecv):
+        t = scores(q_at, k, bias[:, NEAR * TOK :], h)
+        top = jnp.max(t, axis=-1, keepdims=True)
+        p = jnp.exp2(t - top).astype(jnp.bfloat16)
+        acc_at[h] = jnp.dot(p, v, preferred_element_type=jnp.float32)
+        top_at[h] = jnp.broadcast_to(top, (TOK, HEAD))
+
+
+def attend_far(q_at, kv_at, bias, acc_at, top_at, out_at):
+    k, v = keys_values(kv_at, 0, NEAR)
+    for h in range(RATIO):
+        t = scores(q_at, k, bias[:, : NEAR * TOK], h)
+        old = top_at[h]
+        top = jnp.maximum(old, jnp.max(t, axis=-1, keepdims=True))
+        p = jnp.exp2(t - jnp.concatenate([top, top], axis=1)).astype(jnp.bfloat16)
+        fade = jnp.exp2(old - top)
+        acc = acc_at[h] * jnp.concatenate([fade, fade], axis=1) + jnp.dot(p, v, preferred_element_type=jnp.float32)
+        out_at[:, h * HEAD : (h + 1) * HEAD] = (acc[:, :HEAD] / acc[:, HEAD:]).astype(jnp.bfloat16)
+
+
+def first_kernel(n, outer, q_hbm, k_hbm, v_hbm, doc_hbm, part, kv, qv, bias, acc, top, doc, column, tag, mid, in_sem, q_sem, d_sem, send, recv, tsend, trecv, dsend, drecv):
     b = lax.axis_index("inner") * outer + lax.axis_index("outer")
     core = lax.rem(b, 2)
     sibling = b + 1 - 2 * core
@@ -49,6 +71,7 @@
     has_two = b >= 4
     z = lax.rem(b // 2, 8)
     more_rows = b < n - 16
+    ahead = AHEAD + 2 * ((7 - z) // 7)
     is_source = (z == 6) & more_rows
     is_middle = (z == 3) & (b >= 16)
     is_target = (z == 0) & (b >= 16)
@@ -169,13 +192,17 @@
     for g in range(GROUPS):
         for c in load(g):
             c.wait()
-        if g < AHEAD:
-            when(has_next, lambda: move(LINK, g).start())
+        if g < AHEAD + 2:
+            when(has_next & (g < ahead), lambda: move(LINK, g).start())
     for m in range(DIVERT):
         when(is_source, lambda: to_middle(m).start())
     row = lax.broadcasted_iota(jnp.int32, (TOK, TOK), 0)
     col = lax.broadcasted_iota(jnp.int32, (TOK, TOK), 1)
     bias[:, OWN * TOK :] = jnp.where((column[...] == docs) & (col <= row), 0.0, MASKED)
+    def mask(s):
+        other = jnp.broadcast_to(tag[s][:1].astype(jnp.float32), (TOK, TOK))
+        bias[:, s * TOK : (s + 1) * TOK] = jnp.where(column[...] == other, 0.0, MASKED)
+
     def step(it, _):
         @pl.when(it == 0)
         def _():
@@ -191,12 +218,25 @@
             move(PAIR_NEAR, it).start()
             when(core == 0, lambda: move(PAIR_FAR, it).start())
 
-        when(has_next & (it + AHEAD < GROUPS), lambda: move(LINK, it + AHEAD).start())
-
-        @pl.when(is_middle & (it >= KEPT - 1) & (it < GROUPS - 1))
-        def _():
-            to_middle(it - KEPT + 1).wait_recv()
-            from_middle(it - KEPT + 1).start()
+        when(has_next & (it + ahead < GROUPS), lambda: move(LINK, it + ahead).start())
+
+        @pl.when(is_middle & (it < GROUPS))
+        def _():
+            to_middle(it).wait_recv()
+            from_middle(it).start()
+
+        @pl.when(it == 1)
+        def _():
+            move_tag(PAIR_NEAR).wait_recv()
+            mask(2)
+            mask(3)
+
+        @pl.when((it >= 1) & (it < GROUPS + 1))
+        def _():
+            g = it - 1
+            move(PAIR_NEAR, g).wait_recv()
+            load_q(g).wait()
+            attend_near(qv.at[g], kv.at[g], bias, acc.at[g], top.at[g])
 
         @pl.when(it == LAG)
         def _():
@@ -210,19 +250,15 @@
 
         @pl.when(it == LAG + 1)
         def _():
-            move_tag(PAIR_NEAR).wait_recv()
             move_tag(PAIR_FAR).wait_recv()
-            for s in range(OWN):
-                other = jnp.broadcast_to(tag[s][:1].astype(jnp.float32), (TOK, TOK))
-                bias[:, s * TOK : (s + 1) * TOK] = jnp.where(column[...] == other, 0.0, MASKED)
+            mask(0)
+            mask(1)
 
         @pl.when(it > LAG)
         def _():
             g = it - LAG - 1
-            move(PAIR_NEAR, g).wait_recv()
             move(PAIR_FAR, g).wait_recv()
-            load_q(g).wait()
-            attend(qv.at[g], kv.at[g], bias, part.at[g])
+            attend_far(qv.at[g], kv.at[g], bias, acc.at[g], top.at[g], part.at[g])
 
         return 0
 
@@ -248,12 +284,10 @@
         when(is_source, lambda: to_middle(m).wait_send())
         when(is_middle, lambda: from_middle(m).wait_send())
     for g in range(FIRST, GROUPS):
-        load_q(g).wait()
-        move(PAIR_NEAR, g).wait_recv()
         move(PAIR_FAR, g).wait_recv()
 
 
-def last_kernel(part, kv, qv, bias, o_hbm, out, sem):
+def last_kernel(part, kv, qv, bias, acc, top, o_hbm, out, sem):
     def store(g):
         source = part.at[g] if g < FIRST else out.at[g - FIRST]
         return pltpu.make_async_copy(source, o_hbm.at[:, group_columns(g)], sem.at[g])
@@ -261,7 +295,7 @@
     for g in range(FIRST):
         store(g).start()
     for g in range(FIRST, GROUPS):
-        attend(qv.at[g], kv.at[g], bias, out.at[g - FIRST])
+        attend_far(qv.at[g], kv.at[g], bias, acc.at[g], top.at[g], out.at[g - FIRST])
         store(g).start()
     for g in range(GROUPS):
         store(g).wait()
@@ -274,16 +308,18 @@
         anywhere = pl.BlockSpec(memory_space=pl.ANY)
         vmem = pl.BlockSpec(memory_space=pltpu.VMEM)
         arguments = [pltpu.with_memory_space_constraint(x, pltpu.HBM) for x in (queries, keys, values, documents)]
-        part, kv, qv, bias = pl.pallas_call(
+        handed = pl.pallas_call(
             functools.partial(first_kernel, n, outer),
             out_shape=(
                 pltpu.VMEM((FIRST, TOK, RATIO * HEAD), jnp.bfloat16),
                 pltpu.VMEM((GROUPS, 5, 2 * TOK, HEAD), jnp.bfloat16),
                 pltpu.VMEM((GROUPS, TOK, RATIO * HEAD), jnp.bfloat16),
                 pltpu.VMEM((TOK, 5 * TOK), jnp.float32),
+                pltpu.VMEM((GROUPS, RATIO, TOK, 2 * HEAD), jnp.float32),
+                pltpu.VMEM((GROUPS, RATIO, TOK, HEAD), jnp.float32),
             ),
             in_specs=[anywhere] * 4,
-            out_specs=(vmem,) * 4,
+            out_specs=(vmem,) * 6,
             scratch_shapes=[
                 pltpu.VMEM((TOK,), jnp.int32),
                 pltpu.VMEM((TOK, TOK), jnp.float32),
@@ -301,21 +337,21 @@
             ],
             name="relay_and_attend",
             compiler_params=pltpu.CompilerParams(
-                collective_id=0, has_side_effects=True, vmem_limit_bytes=24 * 2**20
+                collective_id=0, has_side_effects=True, vmem_limit_bytes=16 * 2**20
             ),
         )(*arguments)
         return pl.pallas_call(
             last_kernel,
             out_shape=jax.ShapeDtypeStruct(queries.shape, jnp.bfloat16),
-            in_specs=[vmem] * 4,
+            in_specs=[vmem] * 6,
             out_specs=anywhere,
             scratch_shapes=[
                 pltpu.VMEM((GROUPS - FIRST, TOK, RATIO * HEAD), jnp.bfloat16),
                 pltpu.SemaphoreType.DMA((GROUPS,)),
             ],
             name="attend_and_write",
-            compiler_params=pltpu.CompilerParams(vmem_limit_bytes=24 * 2**20),
-        )(part, kv, qv, bias)
+            compiler_params=pltpu.CompilerParams(vmem_limit_bytes=16 * 2**20),
+        )(*handed)
 
     row = P(("inner", "outer"), None)
     return jax.shard_map(local, mesh=mesh, in_specs=(row, row, row, P(("inner", "outer"))), out_specs=row, check_vma=False)

time: 36.9 us -> 32.6 us (0.88)
  the two profiles are of different devices: /device:TPU:38 before, /device:TPU:6 now
where the time goes in v4:
time: 32.6 us; the launch traced here: 32.5 us
  Pallas kernels  32.5 us (100%)
    pallas_call x1, Pallas kernels, local(): pl.pallas_call(functools.partial(first_kernel, n, outer), out_shape=(pltp...  30.9 us
    pallas_call x1, Pallas kernels, local(): pl.pallas_call(last_kernel, out_shape=jax.ShapeDtypeStruct(queries.shape,...  1.59 us

profile of v4, /device:TPU:6, one launch (start us, length us, event | category | flops | bytes accessed | tf_op | source)
XLA Modules:
  0.0 32.5 jit_solution(3074376663654087004)
XLA Ops:
  0.0 30.9 %relay_and_attend.1 = (bf16[7,128,1024]{2,1,0:T(8,128)(2,1)S(1)}, bf16[8,5,256,128]{3,2,1,0:T(8,128)(2,1)S(1)}, bf16[8,128,1024]{2,1,0:T(8,128)(2,1)S(1)}, f32[1...) custom-call(bf16[128,8192]{1,0:T(8,128)(2,1)} %q_hbm.1, ...), custom_call_target="tpu_custom_call" | custom-call | tf_op jit(solution)/shard_map/relay_and_attend/pallas_call | solution.py:311
  30.9 1.6 %attend_and_write.1 = bf16[128,8192]{1,0:T(8,128)(2,1)} custom-call(bf16[7,128,1024]{2,1,0:T(8,128)(2,1)S(1)} %get-tuple-element.11.part, bf16[8,5,256,128]{3,2,1,0:T(8,128)(2,1)S(1)} %get-tuple-element.12.kv, bf16[8,128,1024]{2,1,0:T(8,128)(2,1)S(1)} %get-tuple-element.13.qv, f32[128,640]{1,0:T(8,128)S(1)} %get-tuple-element.14.bias, ...), custom_call_target="tpu_custom_call" | custom-call | tf_op jit(solution)/shard_map/attend_and_write/pallas_call | solution.py:343

commit v5 on v4

--- a/solution.py
+++ b/solution.py
@@ -28,10 +28,17 @@
     return pl.ds(pl.multiple_of(g * RATIO * HEAD, HEAD), RATIO * HEAD)
 
 
+BATCH = 4
+
+
 def scores(q_at, k, bias, h):
-    q = q_at[:, h * HEAD : (h + 1) * HEAD]
-    s = lax.dot_general(q, k, (((1,), (1,)), ((), ())), preferred_element_type=jnp.float32)
-    return s * (HEAD**-0.5 * LOG2E) + bias
+    q, g = q_at
+    q = [q[:, pl.ds(pl.multiple_of((g * RATIO + h + i) * HEAD, HEAD), HEAD)] for i in range(BATCH)]
+    s = lax.dot_general(
+        jnp.concatenate(q, axis=0), k, (((1,), (1,)), ((), ())), preferred_element_type=jnp.float32
+    )
+    t = (s * (HEAD**-0.5 * LOG2E)).reshape(BATCH, TOK, -1) + bias[None]
+    return t.reshape(BATCH * TOK, -1)
 
 
 def keys_values(kv_at, first, last):
@@ -42,27 +49,30 @@
 
 def attend_near(q_at, kv_at, bias, acc_at, top_at):
     k, v = keys_values(kv_at, NEAR, OWN + 1)
-    for h in range(RATIO):
+    for h in range(0, RATIO, BATCH):
         t = scores(q_at, k, bias[:, NEAR * TOK :], h)
         top = jnp.max(t, axis=-1, keepdims=True)
         p = jnp.exp2(t - top).astype(jnp.bfloat16)
-        acc_at[h] = jnp.dot(p, v, preferred_element_type=jnp.float32)
-        top_at[h] = jnp.broadcast_to(top, (TOK, HEAD))
+        acc_at[h : h + BATCH] = jnp.dot(p, v, preferred_element_type=jnp.float32).reshape(BATCH, TOK, 2 * HEAD)
+        top_at[h : h + BATCH] = jnp.broadcast_to(top, (BATCH * TOK, HEAD)).reshape(BATCH, TOK, HEAD)
 
 
 def attend_far(q_at, kv_at, bias, acc_at, top_at, out_at):
     k, v = keys_values(kv_at, 0, NEAR)
-    for h in range(RATIO):
+    for h in range(0, RATIO, BATCH):
         t = scores(q_at, k, bias[:, : NEAR * TOK], h)
-        old = top_at[h]
+        old = top_at[h : h + BATCH].reshape(BATCH * TOK, HEAD)
         top = jnp.maximum(old, jnp.max(t, axis=-1, keepdims=True))
         p = jnp.exp2(t - jnp.concatenate([top, top], axis=1)).astype(jnp.bfloat16)
         fade = jnp.exp2(old - top)
-        acc = acc_at[h] * jnp.concatenate([fade, fade], axis=1) + jnp.dot(p, v, preferred_element_type=jnp.float32)
-        out_at[:, h * HEAD : (h + 1) * HEAD] = (acc[:, :HEAD] / acc[:, HEAD:]).astype(jnp.bfloat16)
-
-
-def first_kernel(n, outer, q_hbm, k_hbm, v_hbm, doc_hbm, part, kv, qv, bias, acc, top, doc, column, tag, mid, in_sem, q_sem, d_sem, send, recv, tsend, trecv, dsend, drecv):
+        acc = acc_at[h : h + BATCH].reshape(BATCH * TOK, 2 * HEAD) * jnp.concatenate([fade, fade], axis=1)
+        acc = acc + jnp.dot(p, v, preferred_element_type=jnp.float32)
+        out = (acc[:, :HEAD] / acc[:, HEAD:]).astype(jnp.bfloat16)
+        for i in range(BATCH):
+            out_at[:, (h + i) * HEAD : (h + i + 1) * HEAD] = out[i * TOK : (i + 1) * TOK]
+
+
+def first_kernel(n, outer, q_hbm, k_hbm, v_hbm, doc_hbm, part, kv, qv, bias, acc, top, kv_in, doc, column, tag, mid, in_sem, q_sem, d_sem, send, recv, tsend, trecv, dsend, drecv):
     b = lax.axis_index("inner") * outer + lax.axis_index("outer")
     core = lax.rem(b, 2)
     sibling = b + 1 - 2 * core
@@ -81,15 +91,9 @@
     def at(device):
         return (device // outer, lax.rem(device, outer))
 
-    def load(g):
-        cols = pl.ds(pl.multiple_of(g * HEAD, HEAD), HEAD)
-        return (
-            pltpu.make_async_copy(k_hbm.at[:, cols], kv.at[g, OWN, pl.ds(0, TOK)], in_sem.at[g, 0]),
-            pltpu.make_async_copy(v_hbm.at[:, cols], kv.at[g, OWN, pl.ds(TOK, TOK)], in_sem.at[g, 1]),
-        )
-
-    def load_q(g):
-        return pltpu.make_async_copy(q_hbm.at[:, group_columns(g)], qv.at[g], q_sem.at[g])
+    load_q = pltpu.make_async_copy(q_hbm, qv, q_sem)
+    load_k = pltpu.make_async_copy(k_hbm, kv_in.at[0], in_sem.at[0])
+    load_v = pltpu.make_async_copy(v_hbm, kv_in.at[1], in_sem.at[1])
 
     near_src = OWN - 2 * core
     far_src = 2 - 2 * core
@@ -145,29 +149,27 @@
     def relays(g):
         return has_prev & has_next & jnp.logical_not((z == 7) & (g >= KEPT))
 
+    barrier = pltpu.get_barrier_semaphore()
+
+    @pl.when(has_prev)
+    def _():
+        pl.semaphore_signal(barrier, inc=1, device_id=at(before), device_id_type=MESH)
+
+    @pl.when(is_middle)
+    def _():
+        pl.semaphore_signal(barrier, inc=1, device_id=at(jnp.maximum(b - 10, 0)), device_id_type=MESH)
+
+    @pl.when(is_target)
+    def _():
+        pl.semaphore_signal(barrier, inc=1, device_id=at(jnp.minimum(b + 6, n - 1)), device_id_type=MESH)
+
+    pl.semaphore_signal(barrier, inc=1, device_id=at(sibling), device_id_type=MESH)
+
     doc_copy = pltpu.make_async_copy(doc_hbm, doc, d_sem)
+    load_k.start()
+    load_v.start()
     doc_copy.start()
-    for g in range(GROUPS):
-        for c in load(g):
-            c.start()
-    for g in range(GROUPS):
-        load_q(g).start()
-
-    barrier = pltpu.get_barrier_semaphore()
-
-    @pl.when(has_prev)
-    def _():
-        pl.semaphore_signal(barrier, inc=1, device_id=at(before), device_id_type=MESH)
-
-    @pl.when(is_middle)
-    def _():
-        pl.semaphore_signal(barrier, inc=1, device_id=at(jnp.maximum(b - 10, 0)), device_id_type=MESH)
-
-    @pl.when(is_target)
-    def _():
-        pl.semaphore_signal(barrier, inc=1, device_id=at(jnp.minimum(b + 6, n - 1)), device_id_type=MESH)
-
-    pl.semaphore_signal(barrier, inc=1, device_id=at(sibling), device_id_type=MESH)
+    load_q.start()
 
     @pl.when(jnp.logical_not(has_two))
     def _():
@@ -179,23 +181,25 @@
         kv[:, 2] = jnp.zeros((GROUPS, 2 * TOK, HEAD), jnp.bfloat16)
         tag[2] = jnp.full((16, TOK), -1, jnp.bfloat16)
 
-    doc_copy.wait()
-    docs = jnp.broadcast_to(doc[...].reshape(1, TOK).astype(jnp.float32), (TOK, TOK))
-    tag[OWN] = docs[:16].astype(jnp.bfloat16)
-    column[...] = docs.T
-
     def when(condition, action):
         pl.when(condition)(action)
 
     pl.semaphore_wait(barrier, 1 + has_next.astype(jnp.int32) + (is_source | is_middle).astype(jnp.int32))
-    when(has_next, lambda: move_tag(LINK).start())
+    load_k.wait()
+    load_v.wait()
     for g in range(GROUPS):
-        for c in load(g):
-            c.wait()
+        for i in range(2):
+            kv[g, OWN, i * TOK : (i + 1) * TOK] = kv_in[i, :, g * HEAD : (g + 1) * HEAD]
         if g < AHEAD + 2:
             when(has_next & (g < ahead), lambda: move(LINK, g).start())
+        if g == 0:
+            doc_copy.wait()
+            docs = jnp.broadcast_to(doc[...].reshape(1, TOK).astype(jnp.float32), (TOK, TOK))
+            tag[OWN] = docs[:16].astype(jnp.bfloat16)
+            when(has_next, lambda: move_tag(LINK).start())
     for m in range(DIVERT):
         when(is_source, lambda: to_middle(m).start())
+    column[...] = docs.T
     row = lax.broadcasted_iota(jnp.int32, (TOK, TOK), 0)
     col = lax.broadcasted_iota(jnp.int32, (TOK, TOK), 1)
     bias[:, OWN * TOK :] = jnp.where((column[...] == docs) & (col <= row), 0.0, MASKED)
@@ -220,13 +224,19 @@
 
         when(has_next & (it + ahead < GROUPS), lambda: move(LINK, it + ahead).start())
 
-        @pl.when(is_middle & (it < GROUPS))
-        def _():
-            to_middle(it).wait_recv()
-            from_middle(it).start()
+        def pass_on(m):
+            to_middle(m).wait_recv()
+            from_middle(m).start()
+
+        @pl.when(is_middle & (it >= 1) & (it < 7))
+        def _():
+            m = it - 1 + (it // 5)
+            pass_on(m)
+            when((it == 4) | (it == 6), lambda: pass_on(m + 1))
 
         @pl.when(it == 1)
         def _():
+            load_q.wait()
             move_tag(PAIR_NEAR).wait_recv()
             mask(2)
             mask(3)
@@ -235,8 +245,7 @@
         def _():
             g = it - 1
             move(PAIR_NEAR, g).wait_recv()
-            load_q(g).wait()
-            attend_near(qv.at[g], kv.at[g], bias, acc.at[g], top.at[g])
+            attend_near((qv, g), kv.at[g], bias, acc.at[g], top.at[g])
 
         @pl.when(it == LAG)
         def _():
@@ -258,7 +267,7 @@
         def _():
             g = it - LAG - 1
             move(PAIR_FAR, g).wait_recv()
-            attend_far(qv.at[g], kv.at[g], bias, acc.at[g], top.at[g], part.at[g])
+            attend_far((qv, g), kv.at[g], bias, acc.at[g], top.at[g], part.at[g])
 
         return 0
 
@@ -295,7 +304,7 @@
     for g in range(FIRST):
         store(g).start()
     for g in range(FIRST, GROUPS):
-        attend_far(qv.at[g], kv.at[g], bias, acc.at[g], top.at[g], out.at[g - FIRST])
+        attend_far((qv, g), kv.at[g], bias, acc.at[g], top.at[g], out.at[g - FIRST])
         store(g).start()
     for g in range(GROUPS):
         store(g).wait()
@@ -313,7 +322,7 @@
             out_shape=(
                 pltpu.VMEM((FIRST, TOK, RATIO * HEAD), jnp.bfloat16),
                 pltpu.VMEM((GROUPS, 5, 2 * TOK, HEAD), jnp.bfloat16),
-                pltpu.VMEM((GROUPS, TOK, RATIO * HEAD), jnp.bfloat16),
+                pltpu.VMEM(queries.shape, jnp.bfloat16),
                 pltpu.VMEM((TOK, 5 * TOK), jnp.float32),
                 pltpu.VMEM((GROUPS, RATIO, TOK, 2 * HEAD), jnp.float32),
                 pltpu.VMEM((GROUPS, RATIO, TOK, HEAD), jnp.float32),
@@ -321,12 +330,13 @@
             in_specs=[anywhere] * 4,
             out_specs=(vmem,) * 6,
             scratch_shapes=[
+                pltpu.VMEM((2, TOK, GROUPS * HEAD), jnp.bfloat16),
                 pltpu.VMEM((TOK,), jnp.int32),
                 pltpu.VMEM((TOK, TOK), jnp.float32),
                 pltpu.VMEM((5, 16, TOK), jnp.bfloat16),
                 pltpu.VMEM((DIVERT, 2 * TOK, HEAD), jnp.bfloat16),
-                pltpu.SemaphoreType.DMA((GROUPS, 2)),
-                pltpu.SemaphoreType.DMA((GROUPS,)),
+                pltpu.SemaphoreType.DMA((2,)),
+                pltpu.SemaphoreType.DMA,
                 pltpu.SemaphoreType.DMA,
                 pltpu.SemaphoreType.DMA((4, GROUPS)),
                 pltpu.SemaphoreType.DMA((4, GROUPS)),

time: 32.6 us -> 31.5 us (0.966)
  Pallas kernels: 32.5 us -> 31.4 us
    pallas_call x1, Pallas kernels: 30.9 us -> 29.9 us  [local(): pl.pallas_call(functools.partial(first_kernel, n, outer), out_shape=(pltp...]
where the time goes in v5:
time: 31.5 us; the launch traced here: 31.4 us
  Pallas kernels  31.4 us (100%)
    pallas_call x1, Pallas kernels, local(): pl.pallas_call(functools.partial(first_kernel, n, outer), out_shape=(pltp...  29.9 us
    pallas_call x1, Pallas kernels, local(): pl.pallas_call(last_kernel, out_shape=jax.ShapeDtypeStruct(queries.shape,...  1.49 us

profile of v5, /device:TPU:6, one launch (start us, length us, event | category | flops | bytes accessed | tf_op | source)
XLA Modules:
  0.0 31.4 jit_solution(4539082225882957563)
XLA Ops:
  0.0 29.9 %relay_and_attend.1 = (bf16[7,128,1024]{2,1,0:T(8,128)(2,1)S(1)}, bf16[8,5,256,128]{3,2,1,0:T(8,128)(2,1)S(1)}, bf16[128,8192]{1,0:T(8,128)(2,1)S(1)}, f32[128,6...) custom-call(bf16[128,8192]{1,0:T(8,128)(2,1)} %q_hbm.1, bf16[128,1024]{1,0:T(8,128)(2,1)} %k_hbm.1, ...), custom_call_target="tpu_custom_call" | custom-call | tf_op jit(solution)/shard_map/relay_and_attend/pallas_call | solution.py:320
  29.9 1.5 %attend_and_write.1 = bf16[128,8192]{1,0:T(8,128)(2,1)} custom-call(bf16[7,128,1024]{2,1,0:T(8,128)(2,1)S(1)} %get-tuple-element.11.part, bf16[8,5,256,128]{3,2,1,0:T(8,128)(2,1)S(1)} %get-tuple-element.12.kv, bf16[128,8192]{1,0:T(8,128)(2,1)S(1)} %get-tuple-element.13.qv, f32[128,640]{1,0:T(8,128)S(1)} %get-tuple-element.14.bias, ...), custom_call_target="tpu_custom_call" | custom-call | tf_op jit(solution)/shard_map/attend_and_write/pallas_call | solution.py:353

commit v6 on v5

--- a/solution.py
+++ b/solution.py
@@ -28,47 +28,50 @@
     return pl.ds(pl.multiple_of(g * RATIO * HEAD, HEAD), RATIO * HEAD)
 
 
-BATCH = 4
-
-
-def scores(q_at, k, bias, h):
+NEAR_BATCH, FAR_BATCH = 8, 2
+
+
+def scores(q_at, k, bias, h, batch):
     q, g = q_at
-    q = [q[:, pl.ds(pl.multiple_of((g * RATIO + h + i) * HEAD, HEAD), HEAD)] for i in range(BATCH)]
+    q = [q[:, pl.ds(pl.multiple_of((g * RATIO + h + i) * HEAD, HEAD), HEAD)] for i in range(batch)]
     s = lax.dot_general(
         jnp.concatenate(q, axis=0), k, (((1,), (1,)), ((), ())), preferred_element_type=jnp.float32
     )
-    t = (s * (HEAD**-0.5 * LOG2E)).reshape(BATCH, TOK, -1) + bias[None]
-    return t.reshape(BATCH * TOK, -1)
+    t = (s * (HEAD**-0.5 * LOG2E)).reshape(batch, TOK, -1) + bias[None]
+    return t.reshape(batch * TOK, -1)
 
 
 def keys_values(kv_at, first, last):
     k = kv_at[first:last, :TOK, :].reshape((last - first) * TOK, HEAD)
     v = kv_at[first:last, TOK:, :].reshape((last - first) * TOK, HEAD)
-    return k, jnp.concatenate([v, jnp.ones_like(v)], axis=1)
+    return k, v
 
 
 def attend_near(q_at, kv_at, bias, acc_at, top_at):
     k, v = keys_values(kv_at, NEAR, OWN + 1)
-    for h in range(0, RATIO, BATCH):
-        t = scores(q_at, k, bias[:, NEAR * TOK :], h)
+    for h in range(0, RATIO, NEAR_BATCH):
+        t = scores(q_at, k, bias[:, NEAR * TOK :], h, NEAR_BATCH)
         top = jnp.max(t, axis=-1, keepdims=True)
-        p = jnp.exp2(t - top).astype(jnp.bfloat16)
-        acc_at[h : h + BATCH] = jnp.dot(p, v, preferred_element_type=jnp.float32).reshape(BATCH, TOK, 2 * HEAD)
-        top_at[h : h + BATCH] = jnp.broadcast_to(top, (BATCH * TOK, HEAD)).reshape(BATCH, TOK, HEAD)
+        p = jnp.exp2(t - top)
+        total = jnp.broadcast_to(jnp.sum(p, axis=-1, keepdims=True), (NEAR_BATCH * TOK, HEAD))
+        acc = jnp.concatenate([jnp.dot(p.astype(jnp.bfloat16), v, preferred_element_type=jnp.float32), total], axis=1)
+        acc_at[h : h + NEAR_BATCH] = acc.reshape(NEAR_BATCH, TOK, 2 * HEAD)
+        top_at[h : h + NEAR_BATCH] = jnp.broadcast_to(top, (NEAR_BATCH * TOK, HEAD)).reshape(NEAR_BATCH, TOK, HEAD)
 
 
 def attend_far(q_at, kv_at, bias, acc_at, top_at, out_at):
     k, v = keys_values(kv_at, 0, NEAR)
-    for h in range(0, RATIO, BATCH):
-        t = scores(q_at, k, bias[:, : NEAR * TOK], h)
-        old = top_at[h : h + BATCH].reshape(BATCH * TOK, HEAD)
+    v = jnp.concatenate([v, jnp.ones_like(v)], axis=1)
+    for h in range(0, RATIO, FAR_BATCH):
+        t = scores(q_at, k, bias[:, : NEAR * TOK], h, FAR_BATCH)
+        old = top_at[h : h + FAR_BATCH].reshape(FAR_BATCH * TOK, HEAD)
         top = jnp.maximum(old, jnp.max(t, axis=-1, keepdims=True))
         p = jnp.exp2(t - jnp.concatenate([top, top], axis=1)).astype(jnp.bfloat16)
         fade = jnp.exp2(old - top)
-        acc = acc_at[h : h + BATCH].reshape(BATCH * TOK, 2 * HEAD) * jnp.concatenate([fade, fade], axis=1)
+        acc = acc_at[h : h + FAR_BATCH].reshape(FAR_BATCH * TOK, 2 * HEAD) * jnp.concatenate([fade, fade], axis=1)
         acc = acc + jnp.dot(p, v, preferred_element_type=jnp.float32)
         out = (acc[:, :HEAD] / acc[:, HEAD:]).astype(jnp.bfloat16)
-        for i in range(BATCH):
+        for i in range(FAR_BATCH):
             out_at[:, (h + i) * HEAD : (h + i + 1) * HEAD] = out[i * TOK : (i + 1) * TOK]
 
 
@@ -192,13 +195,12 @@
             kv[g, OWN, i * TOK : (i + 1) * TOK] = kv_in[i, :, g * HEAD : (g + 1) * HEAD]
         if g < AHEAD + 2:
             when(has_next & (g < ahead), lambda: move(LINK, g).start())
+        when(is_source, lambda: to_middle(g).start())
         if g == 0:
             doc_copy.wait()
             docs = jnp.broadcast_to(doc[...].reshape(1, TOK).astype(jnp.float32), (TOK, TOK))
             tag[OWN] = docs[:16].astype(jnp.bfloat16)
             when(has_next, lambda: move_tag(LINK).start())
-    for m in range(DIVERT):
-        when(is_source, lambda: to_middle(m).start())
     column[...] = docs.T
     row = lax.broadcasted_iota(jnp.int32, (TOK, TOK), 0)
     col = lax.broadcasted_iota(jnp.int32, (TOK, TOK), 1)
@@ -263,7 +265,7 @@
             mask(0)
             mask(1)
 
-        @pl.when(it > LAG)
+        @pl.when((it > LAG) & (it < FIRST + LAG + 1))
         def _():
             g = it - LAG - 1
             move(PAIR_FAR, g).wait_recv()

time: 31.5 us -> 30.6 us (0.971)
  Pallas kernels: 31.4 us -> 30.5 us
    pallas_call x1, Pallas kernels: 29.9 us -> 29 us  [local(): pl.pallas_call(functools.partial(first_kernel, n, outer), out_shape=(pltp...]
where the time goes in v6:
time: 30.6 us; the launch traced here: 30.5 us
  Pallas kernels  30.5 us (100%)
    pallas_call x1, Pallas kernels, local(): pl.pallas_call(functools.partial(first_kernel, n, outer), out_shape=(pltp...  29 us
    pallas_call x1, Pallas kernels, local(): pl.pallas_call(last_kernel, out_shape=jax.ShapeDtypeStruct(queries.shape,...  1.42 us

profile of v6, /device:TPU:6, one launch (start us, length us, event | category | flops | bytes accessed | tf_op | source)
XLA Modules:
  0.0 30.5 jit_solution(243396412451400782)
XLA Ops:
  0.0 29.0 %relay_and_attend.1 = (bf16[7,128,1024]{2,1,0:T(8,128)(2,1)S(1)}, bf16[8,5,256,128]{3,2,1,0:T(8,128)(2,1)S(1)}, bf16[128,8192]{1,0:T(8,128)(2,1)S(1)}, f32[128,6...) custom-call(bf16[128,8192]{1,0:T(8,128)(2,1)} %q_hbm.1, bf16[128,1024]{1,0:T(8,128)(2,1)} %k_hbm.1, ...), custom_call_target="tpu_custom_call" | custom-call | tf_op jit(solution)/shard_map/relay_and_attend/pallas_call | solution.py:322
  29.1 1.4 %attend_and_write.1 = bf16[128,8192]{1,0:T(8,128)(2,1)} custom-call(bf16[7,128,1024]{2,1,0:T(8,128)(2,1)S(1)} %get-tuple-element.11.part, bf16[8,5,256,128]{3,2,1,0:T(8,128)(2,1)S(1)} %get-tuple-element.12.kv, bf16[128,8192]{1,0:T(8,128)(2,1)S(1)} %get-tuple-element.13.qv, f32[128,640]{1,0:T(8,128)S(1)} %get-tuple-element.14.bias, ...), custom_call_target="tpu_custom_call" | custom-call | tf_op jit(solution)/shard_map/attend_and_write/pallas_call | solution.py:355

commit v7 on v6

--- a/solution.py
+++ b/solution.py
@@ -14,8 +14,8 @@
 TOK = 128
 NEAR = 2
 OWN = 4
-AHEAD = 4
-LAG = 3
+AHEAD = 5
+LAG = 4
 DIVERT = 8
 KEPT = GROUPS - DIVERT
 FIRST = GROUPS - 1
@@ -84,7 +84,7 @@
     has_two = b >= 4
     z = lax.rem(b // 2, 8)
     more_rows = b < n - 16
-    ahead = AHEAD + 2 * ((7 - z) // 7)
+    ahead = AHEAD + (7 - z) // 7 - z // 7
     is_source = (z == 6) & more_rows
     is_middle = (z == 3) & (b >= 16)
     is_target = (z == 0) & (b >= 16)

time: 30.6 us -> 30.5 us (level)
  no operation moved by 1% of the time
where the time goes in v7:
time: 30.5 us; the launch traced here: 30.3 us
  Pallas kernels  30.3 us (99%)
    pallas_call x1, Pallas kernels, local(): pl.pallas_call(functools.partial(first_kernel, n, outer), out_shape=(pltp...  28.9 us
    pallas_call x1, Pallas kernels, local(): pl.pallas_call(last_kernel, out_shape=jax.ShapeDtypeStruct(queries.shape,...  1.43 us

profile of v7, /device:TPU:6, one launch (start us, length us, event | category | flops | bytes accessed | tf_op | source)
XLA Modules:
  0.0 30.3 jit_solution(2053068184233917828)
XLA Ops:
  0.0 28.9 %relay_and_attend.1 = (bf16[7,128,1024]{2,1,0:T(8,128)(2,1)S(1)}, bf16[8,5,256,128]{3,2,1,0:T(8,128)(2,1)S(1)}, bf16[128,8192]{1,0:T(8,128)(2,1)S(1)}, f32[128,6...) custom-call(bf16[128,8192]{1,0:T(8,128)(2,1)} %q_hbm.1, bf16[128,1024]{1,0:T(8,128)(2,1)} %k_hbm.1, ...), custom_call_target="tpu_custom_call" | custom-call | tf_op jit(solution)/shard_map/relay_and_attend/pallas_call | solution.py:322
  28.9 1.4 %attend_and_write.1 = bf16[128,8192]{1,0:T(8,128)(2,1)} custom-call(bf16[7,128,1024]{2,1,0:T(8,128)(2,1)S(1)} %get-tuple-element.11.part, bf16[8,5,256,128]{3,2,1,0:T(8,128)(2,1)S(1)} %get-tuple-element.12.kv, bf16[128,8192]{1,0:T(8,128)(2,1)S(1)} %get-tuple-element.13.qv, f32[128,640]{1,0:T(8,128)S(1)} %get-tuple-element.14.bias, ...), custom_call_target="tpu_custom_call" | custom-call | tf_op jit(solution)/shard_map/attend_and_write/pallas_call | solution.py:355
